TPU v7x, 32 devices: a whole 2x2x4 slice. The times are simulated.
32 devices in a mesh: ep: 4 (over z), tp: 4 (over y, x), dp: 2 (over core).
Axes of the slice: x: 2, y: 2, z: 4, core: 2. Of those that a mesh axis runs over, the one named last changes fastest.
Arguments:
- x_in: float32 [16384, 768], P(('ep', 'tp', 'dp')), may hold values from -6 to 6
- grad_out: float32 [16384, 768], P(('ep', 'tp', 'dp')), may hold values from -6 to 6
- norm1_gain: float32 [768], replicated, may hold values from 0.5 to 1.5
- qkv_weight: bfloat16 [768, 2304], P('dp', 'tp'), may hold values from -0.21875 to 0.21875
- out_weight: bfloat16 [768, 768], P('tp', 'dp'), may hold values from -2.5 to 2.5
- bias_table: float32 [32, 12], replicated, may hold values from -4 to 4
- norm2_gain: float32 [768], replicated, may hold values from 0.5 to 1.5
- router_weight: bfloat16 [768, 4], replicated, may hold values from -0.15625 to 0.15625
- expert_in: bfloat16 [4, 768, 3072], P('ep', None, ('tp', 'dp')), may hold values from -0.21875 to 0.21875
- expert_out: bfloat16 [4, 3072, 768], P('ep', ('tp', 'dp')), may hold values from -0.4375 to 0.4375
- lengths: int32 [8, 4], P(('ep', 'dp')), may hold values from 1 to 1024, 2048 in all within a row
- routes: int32 [16384, 1], P(('ep', 'tp', 'dp')), may hold values from 0 to 3; in each aligned block of 512 rows (0 to 511, 512 to 1023, ...) at most 256 rows name the same one
Outputs:
- out: float32 [16384, 768], P(('ep', 'tp', 'dp'))
- grad_in: float32 [16384, 768], P(('ep', 'tp', 'dp'))
- grad_norm1: float32 [768], replicated
- grad_qkv_weight: float32 [768, 2304], P('dp', 'tp')
- grad_out_weight: float32 [768, 768], P('tp', 'dp')
- grad_bias_table: float32 [32, 12], replicated
- grad_norm2: float32 [768], replicated
- grad_router: float32 [768, 4], replicated
- grad_expert_in: float32 [4, 768, 3072], P('ep', None, ('tp', 'dp'))
- grad_expert_out: float32 [4, 3072, 768], P('ep', ('tp', 'dp'))
Inputs may be any that keep to these rules, and one draw needn't show every extreme that they name: `lengths`: each row sums to 2048 and its largest length is exactly 1024. `routes`: within each aligned block of 512 rows (the tokens of one device) no expert is named by more than 256 rows, a bound that some block reaches.
All inputs are finite; a program needn't handle non-finite values.
Results may differ from a plain program's by a relative error of at most 0.023.
Values may be sent and summed in bfloat16 or wider, within the bound.
A program may use at most 192 MiB of HBM per device.

v0:
```python
import jax
import jax.numpy as jnp
from jax import lax
from jax.sharding import PartitionSpec as P

HEAD = 64


EPS = 1e-06
NEG = -1e30
STEP_EDGES = (1, 2, 3, 4, 5, 6, 7, 8, 12, 16, 23, 32, 46, 64, 91)
GELU_C = 0.7978845608028654


def segment_ids(lengths_row, row_count):
    seq_ends = jnp.cumsum(lengths_row, dtype=jnp.int32)
    positions = jnp.arange(row_count, dtype=jnp.int32)
    return jnp.sum(
        (positions[:, None] >= seq_ends[None, :-1]).astype(jnp.int32), axis=1, dtype=jnp.int32
    )


def gelu_tanh(inputs):
    return 0.5 * inputs * (1.0 + jnp.tanh(GELU_C * (inputs + 0.044715 * inputs * inputs * inputs)))


def norm_apply(values, gain_vector):
    return values * lax.rsqrt(jnp.mean(values * values, axis=-1, keepdims=True) + EPS) * gain_vector


def contract_rows(left, right):
    return lax.dot_general(
        left, right, (((0,), (0,)), ((), ())), preferred_element_type=jnp.float32
    )


def contract_cols(left, right):
    return lax.dot_general(
        left, right, (((1,), (1,)), ((), ())), preferred_element_type=jnp.float32
    )


def row_product(left, right, transposed):

    def product(row_start, row_count):
        if transposed:
            return contract_cols(left, right)
        return jnp.dot(left, right, preferred_element_type=jnp.float32)

    return product


def split_columns(values):
    return lax.all_to_all(values, "dp", split_axis=1, concat_axis=0, tiled=True)


def gather_group(values):
    return lax.all_gather(values, "tp", axis=0, tiled=True)


def sum_halves(product, row_count):
    return lax.psum_scatter(
        product(jnp.int32(0), row_count * lax.axis_size("dp")),
        "dp",
        scatter_dimension=0,
        tiled=True,
    )


def gather_halves(values):
    return lax.all_gather(values, "dp", axis=0, tiled=True)


def sum_blocks(product, row_count):
    return lax.psum_scatter(
        product(jnp.int32(0), lax.axis_size("tp") * row_count).astype(jnp.bfloat16),
        "tp",
        scatter_dimension=0,
        tiled=True,
    ).astype(jnp.float32)


def join_rows(values):
    return lax.all_to_all(
        values.astype(jnp.bfloat16), "dp", split_axis=0, concat_axis=1, tiled=True
    ).astype(values.dtype)


def send_experts(values):
    return lax.all_to_all(values, "ep", split_axis=0, concat_axis=0, tiled=True)


def return_tokens(values):
    return lax.all_to_all(values, "ep", split_axis=0, concat_axis=0, tiled=True)


def block_bias(table_heads, row_start, row_count, col_count):
    row_pos = row_start + jnp.arange(row_count, dtype=jnp.int32)
    col_pos = jnp.arange(col_count, dtype=jnp.int32)
    ahead = (col_pos[None, :] > row_pos[:, None])[None]
    far_ahead = table_heads[:, 31][:, None, None]
    far_behind = table_heads[:, 15][:, None, None]
    bias = jnp.where(ahead, far_ahead, far_behind)
    window = min(col_count, row_count + 256)
    win_start = jnp.clip(row_start - 128, 0, col_count - window)
    win_cols = win_start + jnp.arange(window, dtype=jnp.int32)
    offsets = win_cols[None, :] - row_pos[:, None]
    distance = jnp.abs(offsets)
    sign_pos = (offsets > 0)[None]
    diff_behind = table_heads[:, 1:16] - table_heads[:, 0:15]
    diff_ahead = table_heads[:, 17:32] - table_heads[:, 16:31]
    correction = jnp.zeros((table_heads.shape[0], row_count, window), jnp.float32)
    for step_index, edge in enumerate(STEP_EDGES):
        chosen = jnp.where(
            sign_pos,
            diff_ahead[:, step_index][:, None, None],
            diff_behind[:, step_index][:, None, None],
        )
        correction = correction - chosen * (distance < edge)[None].astype(jnp.float32)
    near = lax.dynamic_slice_in_dim(bias, win_start, window, 2) + correction
    return lax.dynamic_update_slice_in_dim(bias, near, win_start, 2)


def attention_forward(
    query_rows, key_rows, value_rows, table_heads, sequence, score_scale, block_rows
):
    group_span = key_rows.shape[0]

    def one_block(row_start):
        rows_here = lax.dynamic_slice_in_dim(query_rows, row_start, block_rows, 0)
        row_seq = lax.dynamic_slice_in_dim(sequence, row_start, block_rows, 0)
        scores = (
            jnp.einsum("qhe,khe->hqk", rows_here, key_rows, preferred_element_type=jnp.float32)
            * score_scale
        )
        scores = scores + block_bias(table_heads, row_start, block_rows, group_span)
        scores = jnp.where((row_seq[:, None] == sequence[None, :])[None], scores, NEG)
        row_max = jnp.max(scores, axis=-1, keepdims=True)
        weights = jnp.exp(scores - row_max)
        row_total = jnp.sum(weights, axis=-1, keepdims=True)
        prob_low = (weights / row_total).astype(jnp.bfloat16)
        output = jnp.einsum(
            "hqk,khe->qhe", prob_low, value_rows, preferred_element_type=jnp.float32
        )
        return (output.astype(jnp.bfloat16), (row_max + jnp.log(row_total))[:, :, 0])

    starts = jnp.arange(group_span // block_rows, dtype=jnp.int32) * block_rows
    outputs, log_sums = lax.map(one_block, starts)
    return (outputs.reshape(group_span, -1), log_sums)


def attention_backward(
    query_rows,
    key_rows,
    value_rows,
    table_heads,
    sequence,
    score_scale,
    block_rows,
    log_sums,
    grad_output,
):
    group_span = key_rows.shape[0]

    def one_block(carry, item):
        grad_keys, grad_values, grad_table = carry
        row_start, row_lse = item
        rows_here = lax.dynamic_slice_in_dim(query_rows, row_start, block_rows, 0)
        row_seq = lax.dynamic_slice_in_dim(sequence, row_start, block_rows, 0)
        grad_rows = lax.dynamic_slice_in_dim(grad_output, row_start, block_rows, 0)
        bias, bias_pull = jax.vjp(
            lambda table_now: block_bias(table_now, row_start, block_rows, group_span), table_heads
        )
        scores = (
            jnp.einsum("qhe,khe->hqk", rows_here, key_rows, preferred_element_type=jnp.float32)
            * score_scale
            + bias
        )
        scores = jnp.where((row_seq[:, None] == sequence[None, :])[None], scores, NEG)
        probs = jnp.exp(scores - row_lse[:, :, None])
        grad_probs = jnp.einsum(
            "qhe,khe->hqk", grad_rows, value_rows, preferred_element_type=jnp.float32
        )
        inner_sum = jnp.sum(probs * grad_probs, axis=-1, keepdims=True)
        grad_scores = (probs * (grad_probs - inner_sum)).astype(jnp.bfloat16)
        prob_low = probs.astype(jnp.bfloat16)
        grad_values = grad_values + jnp.einsum(
            "hqk,qhe->khe", prob_low, grad_rows, preferred_element_type=jnp.float32
        )
        grad_query = (
            jnp.einsum("hqk,khe->qhe", grad_scores, key_rows, preferred_element_type=jnp.float32)
            * score_scale
        )
        grad_keys = (
            grad_keys
            + jnp.einsum("hqk,qhe->khe", grad_scores, rows_here, preferred_element_type=jnp.float32)
            * score_scale
        )
        grad_table = grad_table + bias_pull(grad_scores.astype(jnp.float32))[0]
        return ((grad_keys, grad_values, grad_table), grad_query)

    starts = jnp.arange(group_span // block_rows, dtype=jnp.int32) * block_rows
    zeros_kv = jnp.zeros(key_rows.shape, jnp.float32)
    initial = (zeros_kv, zeros_kv, jnp.zeros(table_heads.shape, jnp.float32))
    (grad_keys, grad_values, grad_table), grad_queries = lax.scan(
        one_block, initial, (starts, log_sums)
    )
    return (grad_queries.reshape(key_rows.shape), grad_keys, grad_values, grad_table)


def shards(
    x_in,
    grad_out,
    norm1_gain,
    qkv_weight,
    out_weight,
    bias_table,
    norm2_gain,
    router_weight,
    expert_in,
    expert_out,
    lengths,
    routes,
):
    tok_rows, model_width = x_in.shape
    heads_local = qkv_weight.shape[1] // (3 * HEAD)
    score_scale = HEAD ** (-0.5)
    tp_count = lax.axis_size("tp")
    dp_count = lax.axis_size("dp")
    normed_f, norm1_pull = jax.vjp(norm_apply, x_in, norm1_gain)
    normed_low = normed_f.astype(jnp.bfloat16)
    group_normed = gather_group(split_columns(normed_low))
    group_total = group_normed.shape[0]
    group_span = group_total // dp_count
    projected = sum_halves(row_product(group_normed, qkv_weight, False), group_span)
    qkv = projected.astype(jnp.bfloat16).reshape(group_span, heads_local, 3, HEAD)
    query_rows, key_rows, value_rows = (qkv[:, :, 0], qkv[:, :, 1], qkv[:, :, 2])
    sequence = segment_ids(lengths[0], group_span)
    head_start = lax.axis_index("tp") * heads_local
    table_heads = jnp.transpose(lax.dynamic_slice_in_dim(bias_table, head_start, heads_local, 1))
    block_rows = min(512, group_span)
    attended, log_sums = attention_forward(
        query_rows, key_rows, value_rows, table_heads, sequence, score_scale, block_rows
    )
    attended_group = gather_halves(attended)
    pair_rows = group_total // tp_count
    attn_cols = sum_blocks(row_product(attended_group, out_weight, False), pair_rows)
    hidden = x_in + join_rows(attn_cols)
    experts_count = lax.axis_size("ep")
    capacity = 2 * tok_rows // experts_count
    normed2_f, norm2_pull = jax.vjp(norm_apply, hidden, norm2_gain)
    normed2 = normed2_f.astype(jnp.bfloat16)
    logits = jnp.dot(normed2, router_weight, preferred_element_type=jnp.float32)
    shifted = jnp.exp(logits - jnp.max(logits, axis=1, keepdims=True))
    router = shifted / jnp.sum(shifted, axis=1, keepdims=True)
    route_int = (routes == jnp.arange(experts_count, dtype=jnp.int32)[None, :]).astype(jnp.int32)
    route_hot = route_int.astype(jnp.float32)
    gate = jnp.sum(router * route_hot, axis=1, keepdims=True)
    earlier = jnp.cumsum(route_int, axis=0) - route_int
    slot_index = jnp.sum(earlier * route_int, axis=1)
    position = routes[:, 0] * capacity + slot_index
    token_ids = jnp.arange(tok_rows, dtype=jnp.int32)
    slot_token = jnp.zeros((experts_count * capacity,), jnp.int32).at[position].set(token_ids)
    slot_live = jnp.zeros((experts_count * capacity, 1), jnp.bfloat16).at[position, 0].set(1.0)
    received = send_experts(jnp.take(normed2, slot_token, axis=0) * slot_live)
    full_in, full_out = (
        lax.all_gather(expert_in, ("tp", "dp"), axis=2, tiled=True),
        lax.all_gather(expert_out, ("tp", "dp"), axis=1, tiled=True),
    )
    pre_act = jnp.dot(received, full_in[0], preferred_element_type=jnp.float32)
    active_f, gelu_pull = jax.vjp(gelu_tanh, pre_act)
    active = active_f.astype(jnp.bfloat16)
    result_f = jnp.dot(active, full_out[0], preferred_element_type=jnp.float32)
    expert_tok = jnp.take(return_tokens(result_f.astype(jnp.bfloat16)), position, axis=0)
    out = hidden + gate * expert_tok.astype(jnp.float32)
    grad_result = (gate * grad_out).astype(jnp.bfloat16)
    grad_gate = jnp.sum(grad_out * expert_tok.astype(jnp.float32), axis=1, keepdims=True)
    grad_received = send_experts(jnp.take(grad_result, slot_token, axis=0) * slot_live)
    grad_active = contract_cols(grad_received, full_out[0])
    grad_pre = gelu_pull(grad_active)[0].astype(jnp.bfloat16)
    grad_first = contract_rows(active, grad_received)
    grad_second = contract_rows(grad_pre, received)
    stacked = lax.psum_scatter(
        jnp.concatenate([grad_first, grad_second], axis=1).astype(jnp.bfloat16),
        ("tp", "dp"),
        scatter_dimension=0,
        tiled=True,
    ).astype(jnp.float32)
    grad_weight_out = stacked[:, :model_width]
    grad_weight_in = jnp.transpose(stacked[:, model_width:])
    grad_sent = contract_cols(grad_pre, full_in[0])
    grad_expert_part = jnp.take(return_tokens(grad_sent.astype(jnp.bfloat16)), position, axis=0)
    grad_router_probs = grad_gate * route_hot
    grad_logits = (
        router * (grad_router_probs - jnp.sum(router * grad_router_probs, axis=1, keepdims=True))
    ).astype(jnp.bfloat16)
    grad_normed2 = grad_expert_part.astype(jnp.float32) + contract_cols(grad_logits, router_weight)
    grad_router = contract_rows(normed2, grad_logits)
    grad_hidden_norm, grad_gain_two = norm2_pull(grad_normed2)
    grad_hidden = grad_out + grad_hidden_norm
    grad_low = grad_hidden.astype(jnp.bfloat16)
    grad_attn_cols = gather_group(split_columns(grad_low))
    grad_out_weight = contract_rows(attended_group, grad_attn_cols)
    grad_attended = sum_halves(row_product(grad_attn_cols, out_weight, True), group_span)
    grad_attended = grad_attended.astype(jnp.bfloat16).reshape(group_span, heads_local, HEAD)
    grad_query, grad_keys, grad_values, grad_table_local = attention_backward(
        query_rows,
        key_rows,
        value_rows,
        table_heads,
        sequence,
        score_scale,
        block_rows,
        log_sums,
        grad_attended,
    )
    grad_qkv = (
        jnp.stack([grad_query, grad_keys, grad_values], axis=2)
        .astype(jnp.bfloat16)
        .reshape(group_span, -1)
    )
    grad_qkv_group = gather_halves(grad_qkv)
    grad_qkv_weight = contract_rows(group_normed, grad_qkv_group)
    grad_normed = join_rows(sum_blocks(row_product(grad_qkv_group, qkv_weight, True), pair_rows))
    grad_x_norm, grad_gain_one = norm1_pull(grad_normed)
    grad_in = grad_hidden + grad_x_norm
    table_full = lax.dynamic_update_slice(
        jnp.zeros(bias_table.shape, jnp.float32),
        jnp.transpose(grad_table_local),
        (jnp.int32(0), head_start),
    )
    grad_qkv_weight, grad_out_weight = (
        lax.psum(grad_qkv_weight.astype(jnp.bfloat16), "ep").astype(jnp.float32),
        lax.psum(grad_out_weight.astype(jnp.bfloat16), "ep").astype(jnp.float32),
    )
    grad_gain_one, grad_gain_two, grad_router, grad_table = lax.psum(
        (grad_gain_one, grad_gain_two, grad_router, table_full), ("ep", "tp", "dp")
    )
    return (
        out,
        grad_in,
        grad_gain_one,
        grad_qkv_weight,
        grad_out_weight,
        grad_table,
        grad_gain_two,
        grad_router,
        grad_weight_in[None],
        grad_weight_out[None],
    )


def solution(mesh):
    placed = (
        P(("ep", "tp", "dp"), None),
        P(("ep", "tp", "dp"), None),
        P(),
        P("dp", "tp"),
        P("tp", "dp"),
        P(),
        P(),
        P(),
        P("ep", None, ("tp", "dp")),
        P("ep", ("tp", "dp"), None),
        P(("ep", "dp"), None),
        P(("ep", "tp", "dp"), None),
    )
    return jax.shard_map(
        shards,
        mesh=mesh,
        in_specs=placed,
        out_specs=(
            P(("ep", "tp", "dp"), None),
            P(("ep", "tp", "dp"), None),
            P(),
            P("dp", "tp"),
            P("tp", "dp"),
            P(),
            P(),
            P(),
            P("ep", None, ("tp", "dp")),
            P("ep", ("tp", "dp"), None),
        ),
        check_vma=False,
    )
```

profile of v0, /device:TPU:0, one launch (start us, length us, event | category | flops | bytes accessed | tf_op | source)
XLA Modules:
  0.0 1808.1 jit_solution(16819961243890486904)
XLA Ops:
  17.2 46.8 %all-gather.7.cloned.1.call-done = bf16[4096,384]{1,0:T(8,128)(2,1)} async-done(((bf16[1024,384]{1,0:T(8,128)(2,1)}), bf16[4096,384]{1,0:T(8,128)(2,1)}) %all-gather.7.cloned.1.call-update) | async-done | bytes 3145744 | tf_op jit(solution)/shard_map/all_gather | solution.py:58
  93.0 279.8 %while.33 = (s32[]{:T(128)}, bf16[4,512,3,64]{1,3,2,0:T(8,128)(2,1)}, f32[4,3,512]{2,1,0:T(4,128)S(1)}, s32[4]{0:T(128)}, s32[2048]{0:T(1024)S(1)}, /*index=5*/b...) while((s32[]{:T(128)}, ...), condition=%wide.region_7.8_spmd, body=%wide.region_4.7_spmd.sunk | while | flops 906198784 | bytes 140199328 | solution.py:148
  127.0 23.3 %dynamic_update_slice.66 = f32[3,512,2048]{2,1,0:T(8,128)} dynamic-update-slice(f32[3,512,2048]{2,1,0:T(8,128)} %broadcast_select_fusion.5, f32[3,512,768]{2,1,0:T(8,128)} %subtract_add_fusion.4, s32[]{:T(128)} %constant.351.clone.1..sunk, s32[]{:T(128)} %constant.351.clone.1..sunk, s32[]{:T(128)S(6)} %min.16) | dynamic-update-slice | bytes 9437188 | tf_op jit(solution)/shard_map/while/body/eval_jaxpr/dynamic_update_slice | solution.py:121
  197.1 23.3 %dynamic_update_slice.66 = f32[3,512,2048]{2,1,0:T(8,128)} dynamic-update-slice(f32[3,512,2048]{2,1,0:T(8,128)} %broadcast_select_fusion.5, f32[3,512,768]{2,1,0:T(8,128)} %subtract_add_fusion.4, s32[]{:T(128)} %constant.351.clone.1..sunk, s32[]{:T(128)} %constant.351.clone.1..sunk, s32[]{:T(128)S(6)} %min.16) | dynamic-update-slice | bytes 9437188 | tf_op jit(solution)/shard_map/while/body/eval_jaxpr/dynamic_update_slice | solution.py:121
  400.9 46.9 %reduce-scatter.10.cloned.1.call-done = bf16[1024,384]{1,0:T(8,128)(2,1)} async-done(((bf16[4096,384]{1,0:T(8,128)(2,1)}), bf16[1024,384]{1,0:T(8,128)(2,1)}) %reduce-scatter.10.cloned.1.call-update) | async-done | bytes 786448 | tf_op jit(solution)/shard_map/reduce_scatter | solution.py:75
  465.5 37.2 %all-to-all-done.2 = bf16[4,256,768]{2,1,0:T(8,128)(2,1)S(1)} async-done(((bf16[4,256,768]{2,1,0:T(8,128)(2,1)}), bf16[4,256,768]{2,1,0:T(8,128)(2,1)S(1)}, u32[]{:S(2)}, u32[]{:S(2)}) %all-to-all-start.2) | async-done | bytes 1572896 | tf_op jit(solution)/shard_map/all_to_all | solution.py:90
  530.0 36.1 %all-to-all-done.3 = bf16[4,256,768]{2,1,0:T(8,128)(2,1)S(1)} async-done(((bf16[4,256,768]{2,1,0:T(8,128)(2,1)}), bf16[4,256,768]{2,1,0:T(8,128)(2,1)S(1)}, u32[]{:S(2)}, u32[]{:S(2)}) %all-to-all-start.3) | async-done | bytes 1572896 | tf_op jit(solution)/shard_map/all_to_all | solution.py:94
  576.2 39.6 %all_to_all.114 = bf16[4,256,768]{2,1,0:T(8,128)(2,1)S(1)} all-to-all(bf16[4,256,768]{2,1,0:T(8,128)(2,1)S(1)} %bitcast.428), channel_id=1, replica_groups=mesh['ep'=4,'tp'=4,'dp'=2] {'ep'}, dimensions={0} | all-to-all | bytes 3145728 | tf_op jit(solution)/shard_map/all_to_all | solution.py:90
  642.6 35.9 %all-to-all-done.5 = bf16[4,256,768]{2,1,0:T(8,128)(2,1)S(1)} async-done(((bf16[4,256,768]{2,1,0:T(8,128)(2,1)}), bf16[4,256,768]{2,1,0:T(8,128)(2,1)S(1)}, u32[]{:S(2)}, u32[]{:S(2)}) %all-to-all-start.5) | async-done | bytes 1572896 | tf_op jit(solution)/shard_map/all_to_all | solution.py:94
  692.1 42.2 %all-gather.15.cloned.1.call-done = bf16[4096,384]{1,0:T(8,128)(2,1)} async-done(((bf16[1024,384]{1,0:T(8,128)(2,1)}), bf16[4096,384]{1,0:T(8,128)(2,1)}) %all-gather.15.cloned.1.call-update) | async-done | bytes 3145744 | tf_op jit(solution)/shard_map/all_gather | solution.py:58
  752.6 790.2 %while.34 = (s32[]{:T(128)}, f32[2048,3,64]{0,2,1:T(8,128)}, f32[2048,3,64]{0,2,1:T(8,128)}, f32[3,32]{0,1:T(8,128)}, bf16[4,512,3,64]{1,3,2,0:T(8,128)(2,1)}, /...) while((s32[]{:T(128)}, f32[2048,3,64]{0,2,1:T(8,128)}, ...), condition=%wide.region_56.59_spmd.clone, body=%wide.region_22.58_spmd.clone.sunk | while | flops 2225833472 | bytes 370949920 | solution.py:205
  801.0 23.3 %dynamic_update_slice.68 = f32[3,512,2048]{2,1,0:T(8,128)} dynamic-update-slice(f32[3,512,2048]{2,1,0:T(8,128)} %broadcast_select_fusion.6, f32[3,512,768]{2,1,0:T(8,128)} %subtract_add_fusion.5, s32[]{:T(128)} %constant.351.clone.1..sunk.1, s32[]{:T(128)} %constant.351.clone.1..sunk.1, s32[]{:T(128)S(6)} %min.17) | dynamic-update-slice | bytes 9437188 | tf_op jit(solution)/shard_map/while/body/eval_jaxpr/jvp()/dynamic_update_slice | solution.py:121
  870.1 23.4 %dynamic_update_slice.69 = f32[3,512,2048]{2,1,0:T(8,128)} dynamic-update-slice(f32[3,512,2048]{2,1,0:T(8,128)} %copy.90, f32[3,512,768]{2,1,0:T(8,128)} %broadcast.1573, s32[]{:T(128)} %constant.351.clone.1..sunk.1, s32[]{:T(128)} %constant.351.clone.1..sunk.1, s32[]{:T(128)S(6)} %min.17) | dynamic-update-slice | bytes 9437188 | tf_op jit(solution)/shard_map/while/body/eval_jaxpr/transpose(jvp())/dynamic_update_slice | solution.py:121
  893.5 24.5 %select_reduce_fusion.34 = (f32[3]{0:T(128)S(1)}, f32[3]{0:T(128)S(1)}, f32[3]{0:T(128)S(1)}, f32[3]{0:T(128)S(1)}, f32[3]{0:T(128)S(1)}, /*index=5*/f32[3]{0:T(...) fusion(f32[512,768]{1,0:T(8,128)} %copy-done.3, ...), kind=kLoop, calls=%fused_computation.125.clone.1 | loop fusion | flops 90832816 | bytes 38142316 | tf_op jit(solution)/shard_map/while/body/eval_jaxpr/transpose(jvp(jit(_where)))/reduce_sum | solution.py:114
  918.0 23.3 %add_any.371 = f32[3,512,2048]{2,1,0:T(8,128)} dynamic-update-slice(f32[3,512,2048]{2,1,0:T(8,128)} %dynamic_update_slice.69, f32[3,512,768]{2,1,0:T(8,128)} %get-tuple-element.1060, s32[]{:T(128)} %constant.351.clone.1..sunk.1, s32[]{:T(128)} %constant.351.clone.1..sunk.1, s32[]{:T(128)S(6)} %min.17) | dynamic-update-slice | bytes 9437188 | tf_op jit(solution)/shard_map/while/body/eval_jaxpr/transpose(jvp())/add_any | solution.py:120
  1068.9 23.3 %dynamic_update_slice.69 = f32[3,512,2048]{2,1,0:T(8,128)} dynamic-update-slice(f32[3,512,2048]{2,1,0:T(8,128)} %copy.90, f32[3,512,768]{2,1,0:T(8,128)} %broadcast.1573, s32[]{:T(128)} %constant.351.clone.1..sunk.1, s32[]{:T(128)} %constant.351.clone.1..sunk.1, s32[]{:T(128)S(6)} %min.17) | dynamic-update-slice | bytes 9437188 | tf_op jit(solution)/shard_map/while/body/eval_jaxpr/transpose(jvp())/dynamic_update_slice | solution.py:121
  1092.2 24.5 %select_reduce_fusion.34 = (f32[3]{0:T(128)S(1)}, f32[3]{0:T(128)S(1)}, f32[3]{0:T(128)S(1)}, f32[3]{0:T(128)S(1)}, f32[3]{0:T(128)S(1)}, /*index=5*/f32[3]{0:T(...) fusion(f32[512,768]{1,0:T(8,128)} %copy-done.3, ...), kind=kLoop, calls=%fused_computation.125.clone.1 | loop fusion | flops 90832816 | bytes 38142316 | tf_op jit(solution)/shard_map/while/body/eval_jaxpr/transpose(jvp(jit(_where)))/reduce_sum | solution.py:114
  1116.7 23.3 %add_any.371 = f32[3,512,2048]{2,1,0:T(8,128)} dynamic-update-slice(f32[3,512,2048]{2,1,0:T(8,128)} %dynamic_update_slice.69, f32[3,512,768]{2,1,0:T(8,128)} %get-tuple-element.1060, s32[]{:T(128)} %constant.351.clone.1..sunk.1, s32[]{:T(128)} %constant.351.clone.1..sunk.1, s32[]{:T(128)S(6)} %min.17) | dynamic-update-slice | bytes 9437188 | tf_op jit(solution)/shard_map/while/body/eval_jaxpr/transpose(jvp())/add_any | solution.py:120
  1290.3 24.5 %select_reduce_fusion.34 = (f32[3]{0:T(128)S(1)}, f32[3]{0:T(128)S(1)}, f32[3]{0:T(128)S(1)}, f32[3]{0:T(128)S(1)}, f32[3]{0:T(128)S(1)}, /*index=5*/f32[3]{0:T(...) fusion(f32[512,768]{1,0:T(8,128)} %copy-done.3, ...), kind=kLoop, calls=%fused_computation.125.clone.1 | loop fusion | flops 90832816 | bytes 38142316 | tf_op jit(solution)/shard_map/while/body/eval_jaxpr/transpose(jvp(jit(_where)))/reduce_sum | solution.py:114
  1486.7 24.5 %select_reduce_fusion.34 = (f32[3]{0:T(128)S(1)}, f32[3]{0:T(128)S(1)}, f32[3]{0:T(128)S(1)}, f32[3]{0:T(128)S(1)}, f32[3]{0:T(128)S(1)}, /*index=5*/f32[3]{0:T(...) fusion(f32[512,768]{1,0:T(8,128)} %copy-done.3, ...), kind=kLoop, calls=%fused_computation.125.clone.1 | loop fusion | flops 90832816 | bytes 38142316 | tf_op jit(solution)/shard_map/while/body/eval_jaxpr/transpose(jvp(jit(_where)))/reduce_sum | solution.py:114
  1606.0 56.2 %reduce-scatter.16.cloned.1.call-done = bf16[384,1536]{1,0:T(8,128)(2,1)} async-done(((bf16[3072,1536]{1,0:T(8,128)(2,1)}), bf16[384,1536]{1,0:T(8,128)(2,1)}) %reduce-scatter.16.cloned.1.call-update) | async-done | bytes 1179664
  1666.6 38.5 %all-reduce.41.cloned.1.call-done = (bf16[384,576]{0,1:T(8,128)(2,1)}, bf16[192,384]{1,0:T(8,128)(2,1)}) async-done(((bf16[384,576]{0,1:T(8,128)(2,1)}, bf16[192,384]{1,0:T(8,128)(2,1)}), (bf16[384,576]{0,1:T(8,128)(2,1)}, bf16[192,384]{1,0:T(8,128)(2,1)})) %all-reduce.41.cloned.1.call-update) | async-done | bytes 589840 | tf_op jit(solution)/shard_map/psum | solution.py:333
  1708.8 43.0 %reduce-scatter.14.cloned.1.call-done = bf16[1024,384]{1,0:T(8,128)(2,1)} async-done(((bf16[4096,384]{1,0:T(8,128)(2,1)}), bf16[1024,384]{1,0:T(8,128)(2,1)}) %reduce-scatter.14.cloned.1.call-update) | async-done | bytes 786448 | tf_op jit(solution)/shard_map/reduce_scatter | solution.py:75
  1760.1 40.2 %all-reduce.37 = (f32[768]{0:T(1024)}, f32[32,12]{0,1:T(8,128)}, f32[768]{0:T(1024)}, f32[768,4]{0,1:T(4,128)}) all-reduce(f32[768]{0:T(1024)S(1)} %get-tuple-element.468, f32[32,12]{0,1:T(8,128)S(1)} %dynamic_update_slice.47, f32[768]{0:T(1024)S(1)} %copy-done.53, ...), channel_id=1, replica_groups=mesh['ep'=4,'tp'=4,'dp'=2] {'ep','tp','dp'}, use_global_device_ids=true, to_apply=%region_60.63 | all-reduce | flops 4992 | bytes 39936 | tf_op jit(solution)/shard_map/psum | solution.py:336
  (555 shorter events, 1044.9 us)
Async XLA Ops:
  8.0 56.0 %copy-start = (bf16[384,576]{0,1:T(8,128)(2,1)S(1)}, bf16[384,576]{0,1:T(8,128)(2,1)}, u32[]{:S(2)}) copy-start(bf16[384,576]{0,1:T(8,128)(2,1)} %param.23) | copy-start | bytes 1327108
  8.0 56.0 %all-gather.7.cloned.1.call-start = ((), (), s32[]{:S(2)}) async-start(), calls=%async_computation.13 | async-start | bytes 3932160 | tf_op jit(solution)/shard_map/all_gather | solution.py:58
  17.1 71.7 %reduce-scatter.8.cloned.1.call-start = ((), (), s32[]{:S(2)}) async-start(), calls=%async_computation.14 | async-start | bytes 14155776 | tf_op jit(solution)/shard_map/reduce_scatter | solution.py:62
  70.9 316.3 %all-gather.9.cloned.1.call-start = ((), (), s32[]{:S(2)}) async-start(), calls=%async_computation.15 | async-start | bytes 2359296 | tf_op jit(solution)/shard_map/all_gather | solution.py:71
  93.0 294.2 %copy-start.37 = (bf16[192,384]{1,0:T(8,128)(2,1)S(1)}, bf16[192,384]{1,0:T(8,128)(2,1)}, u32[]{:S(2)}) copy-start(bf16[192,384]{1,0:T(8,128)(2,1)} %param.24) | copy-start | bytes 442372
  376.0 71.8 %reduce-scatter.10.cloned.1.call-start = ((), (), s32[]{:S(2)}) async-start(), calls=%async_computation.16 | async-start | bytes 3932160 | tf_op jit(solution)/shard_map/reduce_scatter | solution.py:75
  391.6 61.9 %copy-start.15 = (f32[512,768]{1,0:T(8,128)S(1)}, f32[512,768]{1,0:T(8,128)}, u32[]{:S(2)}) copy-start(f32[512,768]{1,0:T(8,128)} %param.20) | copy-start | bytes 4718596
  391.6 73.9 %all-gather.11.cloned.1.call-start = ((), (), s32[]{:S(2)}) async-start(), calls=%async_computation.17 | async-start | bytes 5308416 | tf_op jit(solution)/shard_map/all_gather | solution.py:267
  392.2 121.3 %all-gather.13.cloned.1.call-start = ((), (), s32[]{:S(2)}) async-start(), calls=%async_computation.18 | async-start | bytes 5308416 | tf_op jit(solution)/shard_map/all_gather | solution.py:268
  455.2 74.5 %copy-start.7 = (bf16[512,768]{1,0:T(8,128)(2,1)}, bf16[512,768]{1,0:T(8,128)(2,1)S(1)}, u32[]{:S(2)}) copy-start(bf16[512,768]{1,0:T(8,128)(2,1)S(1)} %multiply_convert_fusion.3) | copy-start | bytes 2359300
  460.7 42.0 %all-to-all-start.2 = ((bf16[4,256,768]{2,1,0:T(8,128)(2,1)}), bf16[4,256,768]{2,1,0:T(8,128)(2,1)S(1)}, u32[]{:S(2)}, u32[]{:S(2)}) async-start(bf16[4,256,768]{2,1,0:T(8,128)(2,1)} %bitcast.52), calls=%async_computation.4 | async-start | bytes 3145728 | tf_op jit(solution)/shard_map/all_to_all | solution.py:90
  526.0 40.1 %all-to-all-start.3 = ((bf16[4,256,768]{2,1,0:T(8,128)(2,1)}), bf16[4,256,768]{2,1,0:T(8,128)(2,1)S(1)}, u32[]{:S(2)}, u32[]{:S(2)}) async-start(bf16[4,256,768]{2,1,0:T(8,128)(2,1)} %bitcast.442), calls=%async_computation.5 | async-start | bytes 3145728 | tf_op jit(solution)/shard_map/all_to_all | solution.py:94
  576.2 56.5 %slice-start = ((s8[4718592]{0:T(1024)(128)(4,1)}), s8[4194304]{0:T(1024)(128)(4,1)S(1)}, s32[]{:S(2)}) async-start(s8[4718592]{0:T(1024)(128)(4,1)} %bitcast.490), calls=%async_computation.25 | async-start | bytes 8388608
  639.0 39.6 %all-to-all-start.5 = ((bf16[4,256,768]{2,1,0:T(8,128)(2,1)}), bf16[4,256,768]{2,1,0:T(8,128)(2,1)S(1)}, u32[]{:S(2)}, u32[]{:S(2)}) async-start(bf16[4,256,768]{2,1,0:T(8,128)(2,1)} %bitcast.443), calls=%async_computation.7 | async-start | bytes 3145728 | tf_op jit(solution)/shard_map/all_to_all | solution.py:94
  642.6 91.7 %all-gather.15.cloned.1.call-start = ((), (), s32[]{:S(2)}) async-start(), calls=%async_computation.19 | async-start | bytes 3932160 | tf_op jit(solution)/shard_map/all_gather | solution.py:58
  642.6 41.8 %copy-start.46 = (bf16[512,4]{0,1:T(4,128)(2,1)}, bf16[512,4]{0,1:T(4,128)(2,1)S(1)}, u32[]{:S(2)}) copy-start(bf16[512,4]{0,1:T(4,128)(2,1)S(1)} %fusion.122) | copy-start | bytes 12292
  692.0 58.2 %reduce-scatter.12.cloned.1.call-start = ((), (), s32[]{:S(2)}) async-start(), calls=%async_computation.20 | async-start | bytes 4718592 | tf_op jit(solution)/shard_map/reduce_scatter | solution.py:62
  739.2 850.3 %all-gather.17.cloned.1.call-start = ((), (), s32[]{:S(2)}) async-start(), calls=%async_computation.21 | async-start | bytes 7077888 | tf_op jit(solution)/shard_map/all_gather | solution.py:71
  1549.1 113.1 %reduce-scatter.16.cloned.1.call-start = ((), (), s32[]{:S(2)}) async-start(), calls=%async_computation.23 | async-start | bytes 10616832
  1584.6 120.6 %all-reduce.41.cloned.1.call-start = ((), (), s32[]{:S(2)}) async-start(), calls=%async_computation.24 | async-start | bytes 1179648 | tf_op jit(solution)/shard_map/psum | solution.py:333
  1597.0 154.7 %reduce-scatter.14.cloned.1.call-start = ((), (), s32[]{:S(2)}) async-start(), calls=%async_computation.22 | async-start | bytes 3932160 | tf_op jit(solution)/shard_map/reduce_scatter | solution.py:75
  1666.6 90.8 %copy-start.16 = (f32[512,768]{1,0:T(8,128)S(1)}, f32[512,768]{1,0:T(8,128)}, u32[]{:S(2)}) copy-start(f32[512,768]{1,0:T(8,128)} %param.20) | copy-start | bytes 4718596
  1666.6 90.8 %copy-start.45 = (f32[768]{0:T(1024)S(1)}, f32[768]{0:T(1024)}, u32[]{:S(2)}) copy-start(f32[768]{0:T(1024)} %param.22) | copy-start | bytes 9220
  1666.6 90.8 %copy-start.49 = (f32[512]{0:T(512)S(1)}, f32[512]{0:T(512)}, u32[]{:S(2)}) copy-start(f32[512]{0:T(512)} %copy-done.48) | copy-start | bytes 6148
  (121 other events, 1228.6 us)
Sparse Core Ops, SparseCore 0:
  17.3 46.6 all-gather.6
  71.1 17.7 reduce-scatter.7
  376.1 11.0 all-gather.8
  391.7 55.9 reduce-scatter.9
  692.1 42.0 all-gather.14
  739.3 10.8 reduce-scatter.11
  1549.2 15.5 all-gather.16
Sparse Core Ops, SparseCore 1:
  394.0 46.9 all-gather.10
  442.7 38.7 all-gather.12
  1584.7 77.5 reduce-scatter.15
  1665.4 39.7 all-reduce.40
  1708.4 43.3 reduce-scatter.13
where the time goes:
time: 1820 us; the launch traced here: 1810 us
  local copies, waits for them, and re-layouts  509 us (28%)
  other arithmetic  460 us (25%)
  waiting for transfers between devices  421 us (23%)
  matrix products  264 us (15%)
  blocking collectives  101 us (6%)
  loops' own time  22.8 us (1%)
    dynamic_update_slice x12, local copies, waits for them, and re-layouts, block_bias(): return lax.dynamic_update_slice_in_dim(bias, near, win_start, 2)  276 us
    add x8, other arithmetic, block_bias(): near = lax.dynamic_slice_in_dim(bias, win_start, window, 2) + correction  118 us
    reduce_sum x4, other arithmetic, block_bias(): jnp.where(sign_pos, diff_ahead[:, step_index][:, None, None], diff_behind...  98 us
    add_any x4, local copies, waits for them, and re-layouts, block_bias(): near = lax.dynamic_slice_in_dim(bias, win_start, window, 2) + correction  92.1 us
    reduce_scatter x2, waiting for transfers between devices, sum_blocks(): lax.psum_scatter(product(jnp.int32(0), lax.axis_size('tp') * row_count).a...  89.9 us
    all_gather x2, waiting for transfers between devices, gather_group(): return lax.all_gather(values, 'tp', axis=0, tiled=True)  89 us
    dot_general x8, matrix products, one_block(): jnp.einsum('qhe,khe->hqk', rows_here, key_rows, preferred_element_type=jn...  72.5 us
    all_to_all x2, waiting for transfers between devices, return_tokens(): return lax.all_to_all(values, 'ep', split_axis=0, concat_axis=0, tiled=True)  72 us
  transfers between devices with their start and end apart: 15, of which 12 were waited for; matrix products, arithmetic and copies ran while one was open for 5% of the time, Pallas kernels for 0%

commit v1 on v0

--- a/solution.py
+++ b/solution.py
@@ -1,6 +1,10 @@
+import functools
+
 import jax
 import jax.numpy as jnp
 from jax import lax
+from jax.experimental import pallas as pl
+from jax.experimental.pallas import tpu as pltpu
 from jax.sharding import PartitionSpec as P
 
 HEAD = 64
@@ -94,118 +98,289 @@
     return lax.all_to_all(values, "ep", split_axis=0, concat_axis=0, tiled=True)
 
 
-def block_bias(table_heads, row_start, row_count, col_count):
-    row_pos = row_start + jnp.arange(row_count, dtype=jnp.int32)
-    col_pos = jnp.arange(col_count, dtype=jnp.int32)
-    ahead = (col_pos[None, :] > row_pos[:, None])[None]
-    far_ahead = table_heads[:, 31][:, None, None]
-    far_behind = table_heads[:, 15][:, None, None]
-    bias = jnp.where(ahead, far_ahead, far_behind)
-    window = min(col_count, row_count + 256)
-    win_start = jnp.clip(row_start - 128, 0, col_count - window)
-    win_cols = win_start + jnp.arange(window, dtype=jnp.int32)
-    offsets = win_cols[None, :] - row_pos[:, None]
+def rel_bucket(offsets):
     distance = jnp.abs(offsets)
-    sign_pos = (offsets > 0)[None]
-    diff_behind = table_heads[:, 1:16] - table_heads[:, 0:15]
-    diff_ahead = table_heads[:, 17:32] - table_heads[:, 16:31]
-    correction = jnp.zeros((table_heads.shape[0], row_count, window), jnp.float32)
-    for step_index, edge in enumerate(STEP_EDGES):
-        chosen = jnp.where(
-            sign_pos,
-            diff_ahead[:, step_index][:, None, None],
-            diff_behind[:, step_index][:, None, None],
+    bucket = jnp.where(offsets > 0, 16, 0)
+    for edge in STEP_EDGES:
+        bucket = bucket + (distance >= edge).astype(jnp.int32)
+    return bucket
+
+
+def tile_offsets(block_rows):
+    keys = jnp.arange(3 * block_rows, dtype=jnp.int32)[:, None] - block_rows
+    return keys - jnp.arange(block_rows, dtype=jnp.int32)[None, :]
+
+
+def bias_tiles(table_heads, block_rows):
+    offsets = tile_offsets(block_rows)[None]
+    distance = jnp.abs(offsets)
+    ahead = offsets > 0
+    near = jnp.zeros((1, 1, 1), jnp.float32) + table_heads[:, 0][:, None, None]
+    for index, edge in enumerate(STEP_EDGES):
+        step = jnp.where(
+            ahead,
+            table_heads[:, 17 + index][:, None, None],
+            table_heads[:, 1 + index][:, None, None],
         )
-        correction = correction - chosen * (distance < edge)[None].astype(jnp.float32)
-    near = lax.dynamic_slice_in_dim(bias, win_start, window, 2) + correction
-    return lax.dynamic_update_slice_in_dim(bias, near, win_start, 2)
-
-
-def attention_forward(
-    query_rows, key_rows, value_rows, table_heads, sequence, score_scale, block_rows
+        near = jnp.where(distance >= edge, step, near)
+    heads = table_heads.shape[0]
+    flat = jnp.ones((1, block_rows, block_rows), jnp.float32)
+    return jnp.concatenate(
+        [
+            table_heads[:, 15][:, None, None] * flat,
+            near,
+            table_heads[:, 31][:, None, None] * flat,
+        ],
+        axis=1,
+    ).reshape(heads, 5, block_rows, block_rows)
+
+
+def table_gradient(tile_sums, block_rows):
+    heads = tile_sums.shape[0]
+    near = tile_sums[:, 1:4].reshape(heads, 3 * block_rows, block_rows)
+    buckets = rel_bucket(tile_offsets(block_rows))
+    sums = [
+        jnp.sum(jnp.where(buckets[None] == index, near, 0.0), axis=(1, 2))
+        for index in range(32)
+    ]
+    sums[15] = sums[15] + jnp.sum(tile_sums[:, 0], axis=(1, 2))
+    sums[31] = sums[31] + jnp.sum(tile_sums[:, 4], axis=(1, 2))
+    return jnp.stack(sums, axis=1)
+
+
+def tile_ranges(lengths_row, sequence, block_rows):
+    ends = jnp.cumsum(lengths_row, dtype=jnp.int32)
+    begins = ends - lengths_row
+    first = jnp.take(begins, sequence[::block_rows]) // block_rows
+    last = (jnp.take(ends, sequence[block_rows - 1 :: block_rows]) + block_rows - 1) // block_rows
+    return jnp.stack([first, last])
+
+
+def attention_forward_kernel(
+    heads, rows, ranges, qkv_t, qkv, seq_col, seq_row, tiles, out, out_t, log_sums, keys
 ):
-    group_span = key_rows.shape[0]
-
-    def one_block(row_start):
-        rows_here = lax.dynamic_slice_in_dim(query_rows, row_start, block_rows, 0)
-        row_seq = lax.dynamic_slice_in_dim(sequence, row_start, block_rows, 0)
-        scores = (
-            jnp.einsum("qhe,khe->hqk", rows_here, key_rows, preferred_element_type=jnp.float32)
-            * score_scale
+    span = qkv.shape[0]
+    blocks = span // rows
+
+    def stage(block, carry):
+        at = pl.ds(pl.multiple_of(block * rows, rows), rows)
+        for head in range(heads):
+            keys[head, at, :] = qkv[at, head * 192 + 64 : head * 192 + 128]
+        return carry
+
+    lax.fori_loop(0, blocks, stage, 0)
+
+    def query_block(block, carry):
+        at = pl.ds(pl.multiple_of(block * rows, rows), rows)
+        own_seq = seq_row[:, at]
+        queries = [qkv_t[head * 192 : head * 192 + 64, at] for head in range(heads)]
+
+        def key_block(other, state):
+            there = pl.ds(pl.multiple_of(other * rows, rows), rows)
+            same = seq_col[there, :] == own_seq
+            kind = jnp.clip(other - block, -2, 2) + 2
+            result = []
+            for head in range(heads):
+                top, total, acc = state[head]
+                scores = jnp.dot(
+                    keys[head, there, :], queries[head], preferred_element_type=jnp.float32
+                )
+                scores = jnp.where(same, scores + tiles[head, kind], NEG)
+                top_now = jnp.maximum(top, jnp.max(scores, axis=0, keepdims=True))
+                weights = jnp.exp(scores - top_now)
+                shrink = jnp.exp(top - top_now)
+                total = total * shrink + jnp.sum(weights, axis=0, keepdims=True)
+                acc = acc * shrink + jnp.dot(
+                    qkv_t[head * 192 + 128 : head * 192 + 192, there],
+                    weights.astype(jnp.bfloat16),
+                    preferred_element_type=jnp.float32,
+                )
+                result.append((top_now, total, acc))
+            return tuple(result)
+
+        initial = tuple(
+            (
+                jnp.full((1, rows), NEG, jnp.float32),
+                jnp.zeros((1, rows), jnp.float32),
+                jnp.zeros((64, rows), jnp.float32),
+            )
+            for head in range(heads)
         )
-        scores = scores + block_bias(table_heads, row_start, block_rows, group_span)
-        scores = jnp.where((row_seq[:, None] == sequence[None, :])[None], scores, NEG)
-        row_max = jnp.max(scores, axis=-1, keepdims=True)
-        weights = jnp.exp(scores - row_max)
-        row_total = jnp.sum(weights, axis=-1, keepdims=True)
-        prob_low = (weights / row_total).astype(jnp.bfloat16)
-        output = jnp.einsum(
-            "hqk,khe->qhe", prob_low, value_rows, preferred_element_type=jnp.float32
+        state = lax.fori_loop(ranges[0, block], ranges[1, block], key_block, initial)
+        for head in range(heads):
+            top, total, acc = state[head]
+            values = acc / total
+            out_t[head * 64 : head * 64 + 64, at] = values
+            log_sums[head, :, at] = top + jnp.log(total)
+        joined = jnp.concatenate(
+            [jnp.transpose(state[head][2] / state[head][1]) for head in range(heads)], axis=1
         )
-        return (output.astype(jnp.bfloat16), (row_max + jnp.log(row_total))[:, :, 0])
-
-    starts = jnp.arange(group_span // block_rows, dtype=jnp.int32) * block_rows
-    outputs, log_sums = lax.map(one_block, starts)
-    return (outputs.reshape(group_span, -1), log_sums)
+        out[at, :] = joined.astype(jnp.bfloat16)
+        return carry
+
+    lax.fori_loop(0, blocks, query_block, 0)
+
+
+def attention_backward_kernel(
+    heads, rows, ranges, qkv_t, qkv, grad_t, grad, out_t, log_sums, seq_col, seq_row, tiles,
+    grad_qkv, tile_sums, parts, grads, grad_q, grad_k, grad_v,
+):
+    span = qkv.shape[0]
+    blocks = span // rows
+    tile_sums[...] = jnp.zeros_like(tile_sums)
+    grad_k[...] = jnp.zeros_like(grad_k)
+    grad_v[...] = jnp.zeros_like(grad_v)
+
+    def stage(block, carry):
+        at = pl.ds(pl.multiple_of(block * rows, rows), rows)
+        for head in range(heads):
+            for kind in range(3):
+                start = head * 192 + kind * 64
+                parts[head, kind, at, :] = qkv[at, start : start + 64]
+            grads[head, at, :] = grad[at, head * 64 : head * 64 + 64]
+        return carry
+
+    lax.fori_loop(0, blocks, stage, 0)
+
+    def query_block(block, carry):
+        at = pl.ds(pl.multiple_of(block * rows, rows), rows)
+        own_seq = seq_row[:, at]
+        inner = [
+            jnp.sum(
+                out_t[head * 64 : head * 64 + 64, at]
+                * grad_t[head * 64 : head * 64 + 64, at].astype(jnp.float32),
+                axis=0,
+                keepdims=True,
+            )
+            for head in range(heads)
+        ]
+        grad_q[...] = jnp.zeros_like(grad_q)
+
+        def key_block(other, state):
+            there = pl.ds(pl.multiple_of(other * rows, rows), rows)
+            same = seq_col[there, :] == own_seq
+            kind = jnp.clip(other - block, -2, 2) + 2
+            for head in range(heads):
+                scores = jnp.dot(
+                    parts[head, 1, there, :],
+                    qkv_t[head * 192 : head * 192 + 64, at],
+                    preferred_element_type=jnp.float32,
+                )
+                scores = jnp.where(same, scores + tiles[head, kind], NEG)
+                probs = jnp.exp(scores - log_sums[head, :, at])
+                grad_probs = jnp.dot(
+                    parts[head, 2, there, :],
+                    grad_t[head * 64 : head * 64 + 64, at],
+                    preferred_element_type=jnp.float32,
+                )
+                grad_scores = probs * (grad_probs - inner[head])
+                tile_sums[head, kind] += grad_scores
+                low_scores = grad_scores.astype(jnp.bfloat16)
+                grad_v[head, there, :] += jnp.dot(
+                    probs.astype(jnp.bfloat16),
+                    grads[head, at, :],
+                    preferred_element_type=jnp.float32,
+                )
+                grad_k[head, there, :] += jnp.dot(
+                    low_scores, parts[head, 0, at, :], preferred_element_type=jnp.float32
+                )
+                grad_q[head] += jnp.dot(
+                    qkv_t[head * 192 + 64 : head * 192 + 128, there],
+                    low_scores,
+                    preferred_element_type=jnp.float32,
+                )
+            return state
+
+        lax.fori_loop(ranges[0, block], ranges[1, block], key_block, 0)
+        for head in range(heads):
+            parts[head, 2 + 1, at, :] = (
+                jnp.transpose(grad_q[head]) * HEAD ** (-0.5)
+            ).astype(jnp.bfloat16)
+        return carry
+
+    lax.fori_loop(0, blocks, query_block, 0)
+
+    def finish(block, carry):
+        at = pl.ds(pl.multiple_of(block * rows, rows), rows)
+        pieces = []
+        for head in range(heads):
+            pieces.append(parts[head, 3, at, :].astype(jnp.float32))
+            pieces.append(grad_k[head, at, :])
+            pieces.append(grad_v[head, at, :])
+        grad_qkv[at, :] = jnp.concatenate(pieces, axis=1).astype(jnp.bfloat16)
+        return carry
+
+    lax.fori_loop(0, blocks, finish, 0)
+
+
+def in_smem():
+    return pl.BlockSpec(memory_space=pltpu.SMEM)
+
+
+def in_vmem(count):
+    return [pl.BlockSpec(memory_space=pltpu.VMEM)] * count
+
+
+def attention_forward(ranges, qkv_t, qkv, sequence, tiles, heads, rows):
+    span = qkv.shape[0]
+    return pl.pallas_call(
+        functools.partial(attention_forward_kernel, heads, rows),
+        out_shape=(
+            jax.ShapeDtypeStruct((span, heads * HEAD), jnp.bfloat16),
+            jax.ShapeDtypeStruct((heads * HEAD, span), jnp.float32),
+            jax.ShapeDtypeStruct((heads, 1, span), jnp.float32),
+        ),
+        in_specs=[in_smem()] + in_vmem(5),
+        out_specs=tuple(in_vmem(3)),
+        scratch_shapes=[pltpu.VMEM((heads, span, HEAD), jnp.bfloat16)],
+        compiler_params=pltpu.CompilerParams(vmem_limit_bytes=48 * 2**20),
+        cost_estimate=pl.CostEstimate(
+            flops=4 * heads * span * span * HEAD,
+            bytes_accessed=12 * 2**20,
+            transcendentals=heads * span * span,
+        ),
+        name="attention_forward",
+    )(ranges, qkv_t, qkv, sequence[:, None], sequence[None, :], tiles)
 
 
 def attention_backward(
-    query_rows,
-    key_rows,
-    value_rows,
-    table_heads,
-    sequence,
-    score_scale,
-    block_rows,
-    log_sums,
-    grad_output,
+    ranges, qkv_t, qkv, grad_output, out_t, log_sums, sequence, tiles, heads, rows
 ):
-    group_span = key_rows.shape[0]
-
-    def one_block(carry, item):
-        grad_keys, grad_values, grad_table = carry
-        row_start, row_lse = item
-        rows_here = lax.dynamic_slice_in_dim(query_rows, row_start, block_rows, 0)
-        row_seq = lax.dynamic_slice_in_dim(sequence, row_start, block_rows, 0)
-        grad_rows = lax.dynamic_slice_in_dim(grad_output, row_start, block_rows, 0)
-        bias, bias_pull = jax.vjp(
-            lambda table_now: block_bias(table_now, row_start, block_rows, group_span), table_heads
-        )
-        scores = (
-            jnp.einsum("qhe,khe->hqk", rows_here, key_rows, preferred_element_type=jnp.float32)
-            * score_scale
-            + bias
-        )
-        scores = jnp.where((row_seq[:, None] == sequence[None, :])[None], scores, NEG)
-        probs = jnp.exp(scores - row_lse[:, :, None])
-        grad_probs = jnp.einsum(
-            "qhe,khe->hqk", grad_rows, value_rows, preferred_element_type=jnp.float32
-        )
-        inner_sum = jnp.sum(probs * grad_probs, axis=-1, keepdims=True)
-        grad_scores = (probs * (grad_probs - inner_sum)).astype(jnp.bfloat16)
-        prob_low = probs.astype(jnp.bfloat16)
-        grad_values = grad_values + jnp.einsum(
-            "hqk,qhe->khe", prob_low, grad_rows, preferred_element_type=jnp.float32
-        )
-        grad_query = (
-            jnp.einsum("hqk,khe->qhe", grad_scores, key_rows, preferred_element_type=jnp.float32)
-            * score_scale
-        )
-        grad_keys = (
-            grad_keys
-            + jnp.einsum("hqk,qhe->khe", grad_scores, rows_here, preferred_element_type=jnp.float32)
-            * score_scale
-        )
-        grad_table = grad_table + bias_pull(grad_scores.astype(jnp.float32))[0]
-        return ((grad_keys, grad_values, grad_table), grad_query)
-
-    starts = jnp.arange(group_span // block_rows, dtype=jnp.int32) * block_rows
-    zeros_kv = jnp.zeros(key_rows.shape, jnp.float32)
-    initial = (zeros_kv, zeros_kv, jnp.zeros(table_heads.shape, jnp.float32))
-    (grad_keys, grad_values, grad_table), grad_queries = lax.scan(
-        one_block, initial, (starts, log_sums)
-    )
-    return (grad_queries.reshape(key_rows.shape), grad_keys, grad_values, grad_table)
+    span = qkv.shape[0]
+    return pl.pallas_call(
+        functools.partial(attention_backward_kernel, heads, rows),
+        out_shape=(
+            jax.ShapeDtypeStruct((span, heads * 3 * HEAD), jnp.bfloat16),
+            jax.ShapeDtypeStruct((heads, 5, rows, rows), jnp.float32),
+        ),
+        in_specs=[in_smem()] + in_vmem(9),
+        out_specs=tuple(in_vmem(2)),
+        scratch_shapes=[
+            pltpu.VMEM((heads, 4, span, HEAD), jnp.bfloat16),
+            pltpu.VMEM((heads, span, HEAD), jnp.bfloat16),
+            pltpu.VMEM((heads, HEAD, rows), jnp.float32),
+            pltpu.VMEM((heads, span, HEAD), jnp.float32),
+            pltpu.VMEM((heads, span, HEAD), jnp.float32),
+        ],
+        compiler_params=pltpu.CompilerParams(vmem_limit_bytes=48 * 2**20),
+        cost_estimate=pl.CostEstimate(
+            flops=10 * heads * span * span * HEAD,
+            bytes_accessed=20 * 2**20,
+            transcendentals=heads * span * span,
+        ),
+        name="attention_backward",
+    )(
+        ranges,
+        qkv_t,
+        qkv,
+        jnp.transpose(grad_output),
+        grad_output,
+        out_t,
+        log_sums,
+        sequence[:, None],
+        sequence[None, :],
+        tiles,
+    )
 
 
 def shards(
@@ -233,14 +408,17 @@
     group_total = group_normed.shape[0]
     group_span = group_total // dp_count
     projected = sum_halves(row_product(group_normed, qkv_weight, False), group_span)
-    qkv = projected.astype(jnp.bfloat16).reshape(group_span, heads_local, 3, HEAD)
-    query_rows, key_rows, value_rows = (qkv[:, :, 0], qkv[:, :, 1], qkv[:, :, 2])
+    kinds = jnp.arange(projected.shape[1], dtype=jnp.int32) // HEAD % 3
+    qkv = (projected * jnp.where(kinds == 0, score_scale, 1.0)[None, :]).astype(jnp.bfloat16)
+    qkv_t = jnp.transpose(qkv)
     sequence = segment_ids(lengths[0], group_span)
     head_start = lax.axis_index("tp") * heads_local
     table_heads = jnp.transpose(lax.dynamic_slice_in_dim(bias_table, head_start, heads_local, 1))
-    block_rows = min(512, group_span)
-    attended, log_sums = attention_forward(
-        query_rows, key_rows, value_rows, table_heads, sequence, score_scale, block_rows
+    block_rows = min(256, group_span)
+    ranges = tile_ranges(lengths[0], sequence, block_rows)
+    tiles = bias_tiles(table_heads, block_rows)
+    attended, attended_t, log_sums = attention_forward(
+        ranges, qkv_t, qkv, sequence, tiles, heads_local, block_rows
     )
     attended_group = gather_halves(attended)
     pair_rows = group_total // tp_count
@@ -302,23 +480,19 @@
     grad_attn_cols = gather_group(split_columns(grad_low))
     grad_out_weight = contract_rows(attended_group, grad_attn_cols)
     grad_attended = sum_halves(row_product(grad_attn_cols, out_weight, True), group_span)
-    grad_attended = grad_attended.astype(jnp.bfloat16).reshape(group_span, heads_local, HEAD)
-    grad_query, grad_keys, grad_values, grad_table_local = attention_backward(
-        query_rows,
-        key_rows,
-        value_rows,
-        table_heads,
+    grad_qkv, tile_sums = attention_backward(
+        ranges,
+        qkv_t,
+        qkv,
+        grad_attended.astype(jnp.bfloat16),
+        attended_t,
+        log_sums,
         sequence,
-        score_scale,
+        tiles,
+        heads_local,
         block_rows,
-        log_sums,
-        grad_attended,
-    )
-    grad_qkv = (
-        jnp.stack([grad_query, grad_keys, grad_values], axis=2)
-        .astype(jnp.bfloat16)
-        .reshape(group_span, -1)
-    )
+    )
+    grad_table_local = table_gradient(tile_sums, block_rows)
     grad_qkv_group = gather_halves(grad_qkv)
     grad_qkv_weight = contract_rows(group_normed, grad_qkv_group)
     grad_normed = join_rows(sum_blocks(row_product(grad_qkv_group, qkv_weight, True), pair_rows))

time: 1820 us -> 826 us (0.45)
  local copies, waits for them, and re-layouts: 509 us -> 57.1 us
  other arithmetic: 460 us -> 67.9 us
  matrix products: 264 us -> 105 us
  Pallas kernels: 0 us -> 81.2 us
  waiting for transfers between devices: 421 us -> 381 us
  loops' own time: 22.8 us -> 0 us
    dynamic_update_slice x12 -> x0, local copies, waits for them, and re-layouts: 276 us -> none  [block_bias(): return lax.dynamic_update_slice_in_dim(bias, near, win_start, 2)]
    dot_general x28 -> x0, matrix products: 160 us -> none  [the longest x8 72.5 us: one_block(): jnp.einsum('qhe,khe->hqk', rows_here, key_rows, preferred_element_type=jn...]
    add x28 -> x2, other arithmetic: 126 us -> 0.01 us  [the longest x1 0.01 us: table_gradient(): sums[15] = sums[15] + jnp.sum(tile_sums[:, 0], axis=(1, 2))]
    reduce_sum x12 -> x4, other arithmetic: 138 us -> 16 us  [the longest x3 14.4 us: table_gradient(): jnp.sum(jnp.where(buckets[None] == index, near, 0.0), axis=(1, 2))]
    add_any x4 -> x0, local copies, waits for them, and re-layouts: 92.1 us -> none  [block_bias(): near = lax.dynamic_slice_in_dim(bias, win_start, window, 2) + correction]
    pallas_call x0 -> x2, Pallas kernels: none -> 81.2 us  [the longest x1 42.2 us: attention_backward(): pl.pallas_call(functools.partial(attention_backward_kernel, heads, rows),...]
    while x198 -> x0, local copies, waits for them, and re-layouts: 64.1 us -> none
    gt x16 -> x0, other arithmetic: 57.7 us -> none  [the longest x8 52.5 us: block_bias(): sign_pos = (offsets > 0)[None]]
  transfers between devices with their start and end apart: 15 -> 15, of which waited for: 12 -> 12; matrix products, arithmetic and copies ran while one was open for 5% -> 16% of each run, Pallas kernels for 0% -> 0%
where the time goes in v1:
time: 826 us; the launch traced here: 823 us
  waiting for transfers between devices  381 us (46%)
  matrix products  105 us (13%)
  blocking collectives  101 us (12%)
  Pallas kernels  81.2 us (10%)
  other arithmetic  67.9 us (8%)
  local copies, waits for them, and re-layouts  57.1 us (7%)
  between operations  16.7 us (2%)
  starting transfers between devices  13.6 us (2%)
    reduce_scatter x2, waiting for transfers between devices, sum_blocks(): lax.psum_scatter(product(jnp.int32(0), lax.axis_size('tp') * row_count).a...  90 us
    all_gather x2, waiting for transfers between devices, gather_group(): return lax.all_gather(values, 'tp', axis=0, tiled=True)  88.8 us
    all_to_all x2, waiting for transfers between devices, return_tokens(): return lax.all_to_all(values, 'ep', split_axis=0, concat_axis=0, tiled=True)  72 us
    pallas_call x1, Pallas kernels, attention_backward(): pl.pallas_call(functools.partial(attention_backward_kernel, heads, rows),...  42.2 us
    psum x1, blocking collectives, shards(): lax.psum((grad_gain_one, grad_gain_two, grad_router, table_full), ('ep',...  40.2 us
    all_to_all x1, blocking collectives, send_experts(): return lax.all_to_all(values, 'ep', split_axis=0, concat_axis=0, tiled=True)  39.2 us
    pallas_call x1, Pallas kernels, attention_forward(): pl.pallas_call(functools.partial(attention_forward_kernel, heads, rows),...  38.9 us
    dot_general x5, matrix products, contract_cols(): lax.dot_general(left, right, (((1,), (1,)), ((), ())), preferred_element_...  38.7 us
  transfers between devices with their start and end apart: 15, of which 12 were waited for; matrix products, arithmetic and copies ran while one was open for 16% of the time, Pallas kernels for 0%

profile of v1, /device:TPU:0, one launch (start us, length us, event | category | flops | bytes accessed | tf_op | source)
XLA Modules:
  0.0 823.5 jit_solution(12636223887221453363)
XLA Ops:
  16.6 46.8 %all-gather.7.cloned.1.call-done = bf16[4096,384]{1,0:T(8,128)(2,1)} async-done(((bf16[1024,384]{1,0:T(8,128)(2,1)}), bf16[4096,384]{1,0:T(8,128)(2,1)}) %all-gather.7.cloned.1.call-update) | async-done | bytes 3145744 | tf_op jit(solution)/shard_map/all_gather | solution.py:62
  63.4 8.9 %fusion.95 = f32[4096,576]{1,0:T(8,128)} fusion(bf16[4096,384]{1,0:T(8,128)(2,1)} %all-gather.7.cloned.1.call-done, bf16[384,576]{0,1:T(8,128)(2,1)S(1)} %copy-done), kind=kOutput, calls=%fused_computation.280 | convolution fusion | flops 1811939328 | bytes 13025280 | tf_op jit(solution)/shard_map/dot_general | solution.py:52
  104.1 38.9 %attention_forward.1 = (bf16[2048,192]{1,0:T(8,128)(2,1)S(1)}, f32[192,2048]{1,0:T(8,128)S(1)}, f32[3,1,2048]{2,1,0:T(1,128)S(1)}) custom-call(s32[2,8]{1,0:T(2,128)S(1)} %pad_add_fusion.ranges, bf16[576,2048]{1,0:T(8,128)(2,1)S(1)} %copy.90.qkv_t, bf16[2048,576]{1,0:T(8,128)(2,1)} %multiply_convert_fusion.1.qkv, s32[2048,1]{1,0:T(8,128)S(1)} %copy-done.2, ...), custom_call_target="tpu_custom_call" | custom-call | flops 3221225472 | bytes 12582912 | tf_op jit(solution)/shard_map/attention_forward/pallas_call | solution.py:326
  145.3 10.1 %all-gather.9.cloned.1.call-done = bf16[4096,192]{1,0:T(8,128)(2,1)} async-done(((bf16[2048,192]{1,0:T(8,128)(2,1)}), bf16[4096,192]{1,0:T(8,128)(2,1)}) %all-gather.9.cloned.1.call-update) | async-done | bytes 1572880 | tf_op jit(solution)/shard_map/all_gather | solution.py:75
  169.1 47.0 %reduce-scatter.10.cloned.1.call-done = bf16[1024,384]{1,0:T(8,128)(2,1)} async-done(((bf16[4096,384]{1,0:T(8,128)(2,1)}), bf16[1024,384]{1,0:T(8,128)(2,1)}) %reduce-scatter.10.cloned.1.call-update) | async-done | bytes 786448 | tf_op jit(solution)/shard_map/reduce_scatter | solution.py:79
  234.7 37.3 %all-to-all-done.2 = bf16[4,256,768]{2,1,0:T(8,128)(2,1)S(1)} async-done(((bf16[4,256,768]{2,1,0:T(8,128)(2,1)}), bf16[4,256,768]{2,1,0:T(8,128)(2,1)S(1)}, u32[]{:S(2)}, u32[]{:S(2)}) %all-to-all-start.2) | async-done | bytes 1572896 | tf_op jit(solution)/shard_map/all_to_all | solution.py:94
  272.0 10.8 %fusion.12 = f32[1024,3072]{1,0:T(8,128)} fusion(bf16[1024,768]{1,0:T(8,128)(2,1)S(1)} %bitcast.167, bf16[1,768,3072]{2,1,0:T(8,128)(2,1)} %all-gather.11.cloned.1.call-done), kind=kOutput, calls=%fused_computation.31 | convolution fusion | flops 4831838208 | bytes 18874368 | tf_op jit(solution)/shard_map/dot_general | solution.py:448
  282.8 12.5 %fusion.19 = bf16[1024,768]{1,0:T(8,128)(2,1)} fusion(bf16[1,3072,768]{2,1,0:T(8,128)(2,1)} %all-gather.13.cloned.1.call-done, f32[1024,3072]{1,0:T(8,128)} %fusion.12), kind=kOutput, calls=%fused_computation.72 | convolution fusion | flops 4860936192 | bytes 18874368 | tf_op jit(solution)/shard_map/dot_general | solution.py:451
  299.9 36.1 %all-to-all-done.3 = bf16[4,256,768]{2,1,0:T(8,128)(2,1)S(1)} async-done(((bf16[4,256,768]{2,1,0:T(8,128)(2,1)}), bf16[4,256,768]{2,1,0:T(8,128)(2,1)S(1)}, u32[]{:S(2)}, u32[]{:S(2)}) %all-to-all-start.3) | async-done | bytes 1572896 | tf_op jit(solution)/shard_map/all_to_all | solution.py:98
  344.6 39.2 %all_to_all.114 = bf16[4,256,768]{2,1,0:T(8,128)(2,1)S(1)} all-to-all(bf16[4,256,768]{2,1,0:T(8,128)(2,1)S(1)} %bitcast.157), channel_id=1, replica_groups=mesh['ep'=4,'tp'=4,'dp'=2] {'ep'}, dimensions={0} | all-to-all | bytes 3145728 | tf_op jit(solution)/shard_map/all_to_all | solution.py:94
  383.9 16.9 %fusion.3 = bf16[1024,3072]{1,0:T(8,128)(2,1)S(1)} fusion(f32[1024,3072]{1,0:T(8,128)} %fusion.12, bf16[1024,768]{1,0:T(8,128)(2,1)S(1)} %bitcast.169, bf16[1,3072,768]{2,1,0:T(8,128)(2,1)} %all-gather.13.cloned.1.call-done), kind=kOutput, calls=%fused_computation.15 | convolution fusion | flops 4907335680 | bytes 25165824 | tf_op jit(solution)/shard_map/dot_general | solution.py:42
  410.7 35.9 %all-to-all-done.5 = bf16[4,256,768]{2,1,0:T(8,128)(2,1)S(1)} async-done(((bf16[4,256,768]{2,1,0:T(8,128)(2,1)}), bf16[4,256,768]{2,1,0:T(8,128)(2,1)S(1)}, u32[]{:S(2)}, u32[]{:S(2)}) %all-to-all-start.5) | async-done | bytes 1572896 | tf_op jit(solution)/shard_map/all_to_all | solution.py:98
  458.9 42.0 %all-gather.15.cloned.1.call-done = bf16[4096,384]{1,0:T(8,128)(2,1)} async-done(((bf16[1024,384]{1,0:T(8,128)(2,1)}), bf16[4096,384]{1,0:T(8,128)(2,1)}) %all-gather.15.cloned.1.call-update) | async-done | bytes 3145744 | tf_op jit(solution)/shard_map/all_gather | solution.py:62
  506.2 12.1 %reduce-scatter.12.cloned.1.call-done = f32[2048,192]{1,0:T(8,128)} async-done(((f32[4096,192]{1,0:T(8,128)}), f32[2048,192]{1,0:T(8,128)}) %reduce-scatter.12.cloned.1.call-update) | async-done | bytes 1572880 | tf_op jit(solution)/shard_map/reduce_scatter | solution.py:66
  522.6 42.2 %attention_backward.1 = (bf16[2048,576]{1,0:T(8,128)(2,1)}, f32[3,5,256,256]{3,2,1,0:T(8,128)}) custom-call(s32[2,8]{1,0:T(2,128)S(1)} %pad_add_fusion.ranges, bf16[576,2048]{1,0:T(8,128)(2,1)} %copy-done.1, bf16[2048,576]{1,0:T(8,128)(2,1)} %multiply_convert_fusion.1.qkv, bf16[192,2048]{1,0:T(8,128)(2,1)S(1)} %copy.96.grad_t, ...), custom_call_target="tpu_custom_call" | custom-call | flops 8053063680 | bytes 20971520 | tf_op jit(solution)/shard_map/attention_backward/pallas_call | solution.py:350
  566.3 8.3 %convolution_convert_fusion.2 = bf16[3072,768]{0,1:T(8,128)(2,1)S(1)} fusion(bf16[1024,3072]{1,0:T(8,128)(2,1)} %copy-done.35, bf16[1024,768]{1,0:T(8,128)(2,1)S(1)} %bitcast.168), kind=kOutput, calls=%fused_computation.23 | convolution fusion | flops 4834197504 | bytes 12582912 | tf_op jit(solution)/shard_map/dot_general | solution.py:36
  574.6 9.5 %convolution_convert_fusion.3 = bf16[3072,768]{0,1:T(8,128)(2,1)S(1)} fusion(bf16[1024,768]{1,0:T(8,128)(2,1)S(1)} %bitcast.170, f32[1024,3072]{1,0:T(8,128)} %fusion.12), kind=kOutput, calls=%fused_computation.24 | convolution fusion | flops 4862509056 | bytes 18874368 | tf_op jit(solution)/shard_map/dot_general | solution.py:36
  588.4 12.7 %copy.134 = bf16[3072,1536]{1,0:T(8,128)(2,1)} copy(bf16[3072,1536]{0,1:T(8,128)(2,1)} %pad_maximum_fusion) | data formatting | bytes 18874368
  606.2 7.9 convolution_convert_fusion.4
  614.4 8.1 convolution_convert_fusion
  648.5 28.5 %reduce-scatter.16.cloned.1.call-done = bf16[384,1536]{1,0:T(8,128)(2,1)} async-done(((bf16[3072,1536]{1,0:T(8,128)(2,1)}), bf16[384,1536]{1,0:T(8,128)(2,1)}) %reduce-scatter.16.cloned.1.call-update) | async-done | bytes 1179664
  681.4 38.5 %all-reduce.5.cloned.1.call-done = (bf16[384,576]{0,1:T(8,128)(2,1)}, bf16[192,384]{1,0:T(8,128)(2,1)}) async-done(((bf16[384,576]{0,1:T(8,128)(2,1)}, bf16[192,384]{1,0:T(8,128)(2,1)}), (bf16[384,576]{0,1:T(8,128)(2,1)}, bf16[192,384]{1,0:T(8,128)(2,1)})) %all-reduce.5.cloned.1.call-update) | async-done | bytes 589840 | tf_op jit(solution)/shard_map/psum | solution.py:507
  723.6 43.0 %reduce-scatter.14.cloned.1.call-done = bf16[1024,384]{1,0:T(8,128)(2,1)} async-done(((bf16[4096,384]{1,0:T(8,128)(2,1)}), bf16[1024,384]{1,0:T(8,128)(2,1)}) %reduce-scatter.14.cloned.1.call-update) | async-done | bytes 786448 | tf_op jit(solution)/shard_map/reduce_scatter | solution.py:79
  775.5 40.2 %all-reduce.1 = (f32[768]{0:T(1024)}, f32[32,12]{0,1:T(8,128)}, f32[768]{0:T(1024)}, f32[768,4]{0,1:T(4,128)}) all-reduce(f32[768]{0:T(1024)S(1)} %get-tuple-element.99, f32[32,12]{0,1:T(8,128)S(1)} %dynamic_update_slice.3, f32[768]{0:T(1024)S(1)} %get-tuple-element.97, ...), channel_id=1, replica_groups=mesh['ep'=4,'tp'=4,'dp'=2] {'ep','tp','dp'}, use_global_device_ids=true, to_apply=%region_21.25 | all-reduce | flops 4992 | bytes 39936 | tf_op jit(solution)/shard_map/psum | solution.py:510
  (243 shorter events, 173.4 us)
Async XLA Ops:
  8.0 55.4 %copy-start = (bf16[384,576]{0,1:T(8,128)(2,1)S(1)}, bf16[384,576]{0,1:T(8,128)(2,1)}, u32[]{:S(2)}) copy-start(bf16[384,576]{0,1:T(8,128)(2,1)} %param.21) | copy-start | bytes 1327108
  8.0 55.3 %all-gather.7.cloned.1.call-start = ((), (), s32[]{:S(2)}) async-start(), calls=%async_computation.13 | async-start | bytes 3932160 | tf_op jit(solution)/shard_map/all_gather | solution.py:62
  16.5 75.0 %reduce-scatter.8.cloned.1.call-start = ((), (), s32[]{:S(2)}) async-start(), calls=%async_computation.14 | async-start | bytes 15728640 | tf_op jit(solution)/shard_map/reduce_scatter | solution.py:66
  72.3 83.0 %all-gather.9.cloned.1.call-start = ((), (), s32[]{:S(2)}) async-start(), calls=%async_computation.15 | async-start | bytes 3145728 | tf_op jit(solution)/shard_map/all_gather | solution.py:75
  104.1 51.2 %copy-start.25 = (bf16[192,384]{1,0:T(8,128)(2,1)S(1)}, bf16[192,384]{1,0:T(8,128)(2,1)}, u32[]{:S(2)}) copy-start(bf16[192,384]{1,0:T(8,128)(2,1)} %param.22) | copy-start | bytes 442372
  145.2 70.9 %reduce-scatter.10.cloned.1.call-start = ((), (), s32[]{:S(2)}) async-start(), calls=%async_computation.16 | async-start | bytes 3932160 | tf_op jit(solution)/shard_map/reduce_scatter | solution.py:79
  159.9 74.8 %all-gather.11.cloned.1.call-start = ((), (), s32[]{:S(2)}) async-start(), calls=%async_computation.17 | async-start | bytes 5308416 | tf_op jit(solution)/shard_map/all_gather | solution.py:445
  160.5 122.3 %all-gather.13.cloned.1.call-start = ((), (), s32[]{:S(2)}) async-start(), calls=%async_computation.18 | async-start | bytes 5308416 | tf_op jit(solution)/shard_map/all_gather | solution.py:446
  224.6 74.9 %copy-start.7 = (bf16[512,768]{1,0:T(8,128)(2,1)}, bf16[512,768]{1,0:T(8,128)(2,1)S(1)}, u32[]{:S(2)}) copy-start(bf16[512,768]{1,0:T(8,128)(2,1)S(1)} %multiply_convert_fusion.3) | copy-start | bytes 2359300
  230.1 41.9 %all-to-all-start.2 = ((bf16[4,256,768]{2,1,0:T(8,128)(2,1)}), bf16[4,256,768]{2,1,0:T(8,128)(2,1)S(1)}, u32[]{:S(2)}, u32[]{:S(2)}) async-start(bf16[4,256,768]{2,1,0:T(8,128)(2,1)} %bitcast.20), calls=%async_computation.4 | async-start | bytes 3145728 | tf_op jit(solution)/shard_map/all_to_all | solution.py:94
  272.0 10.8 %copy-start.21 = (bf16[4,256,768]{2,1,0:T(8,128)(2,1)}, bf16[4,256,768]{2,1,0:T(8,128)(2,1)S(1)}, u32[]{:S(2)}) copy-start(bf16[4,256,768]{2,1,0:T(8,128)(2,1)S(1)} %all-to-all-done.2) | copy-start | bytes 4718596
  295.3 40.6 %all-to-all-start.3 = ((bf16[4,256,768]{2,1,0:T(8,128)(2,1)}), bf16[4,256,768]{2,1,0:T(8,128)(2,1)S(1)}, u32[]{:S(2)}, u32[]{:S(2)}) async-start(bf16[4,256,768]{2,1,0:T(8,128)(2,1)} %bitcast.171), calls=%async_computation.5 | async-start | bytes 3145728 | tf_op jit(solution)/shard_map/all_to_all | solution.py:98
  344.6 56.1 %slice-start = ((s8[4718592]{0:T(1024)(128)(4,1)}), s8[4194304]{0:T(1024)(128)(4,1)S(1)}, s32[]{:S(2)}) async-start(s8[4718592]{0:T(1024)(128)(4,1)} %bitcast.215), calls=%async_computation.25 | async-start | bytes 8388608
  383.9 16.9 %copy-start.23 = (bf16[4,256,768]{2,1,0:T(8,128)(2,1)}, bf16[4,256,768]{2,1,0:T(8,128)(2,1)S(1)}, u32[]{:S(2)}) copy-start(bf16[4,256,768]{2,1,0:T(8,128)(2,1)S(1)} %all_to_all.114) | copy-start | bytes 4718596
  383.9 16.9 %slice-start.1 = ((s8[4718592]{0:T(1024)(128)(4,1)}), s8[524288]{0:T(1024)(128)(4,1)S(1)}, s32[]{:S(2)}) async-start(s8[4718592]{0:T(1024)(128)(4,1)} %bitcast.215), calls=%async_computation.26 | async-start | bytes 1048576
  407.1 39.6 %all-to-all-start.5 = ((bf16[4,256,768]{2,1,0:T(8,128)(2,1)}), bf16[4,256,768]{2,1,0:T(8,128)(2,1)S(1)}, u32[]{:S(2)}, u32[]{:S(2)}) async-start(bf16[4,256,768]{2,1,0:T(8,128)(2,1)} %bitcast.172), calls=%async_computation.7 | async-start | bytes 3145728 | tf_op jit(solution)/shard_map/all_to_all | solution.py:98
  410.6 90.4 %all-gather.15.cloned.1.call-start = ((), (), s32[]{:S(2)}) async-start(), calls=%async_computation.19 | async-start | bytes 3932160 | tf_op jit(solution)/shard_map/all_gather | solution.py:62
  458.7 59.6 %reduce-scatter.12.cloned.1.call-start = ((), (), s32[]{:S(2)}) async-start(), calls=%async_computation.20 | async-start | bytes 6291456 | tf_op jit(solution)/shard_map/reduce_scatter | solution.py:66
  506.1 100.1 %all-gather.17.cloned.1.call-start = ((), (), s32[]{:S(2)}) async-start(), calls=%async_computation.21 | async-start | bytes 7864320 | tf_op jit(solution)/shard_map/all_gather | solution.py:75
  564.9 112.1 %reduce-scatter.16.cloned.1.call-start = ((), (), s32[]{:S(2)}) async-start(), calls=%async_computation.23 | async-start | bytes 10616832
  566.3 8.3 %copy-start.24 = (bf16[4,256,768]{2,1,0:T(8,128)(2,1)S(1)}, bf16[4,256,768]{2,1,0:T(8,128)(2,1)}, u32[]{:S(2)}) copy-start(bf16[4,256,768]{2,1,0:T(8,128)(2,1)} %copy-done.23) | copy-start | bytes 4718596
  601.1 118.8 %all-reduce.5.cloned.1.call-start = ((), (), s32[]{:S(2)}) async-start(), calls=%async_computation.24 | async-start | bytes 1179648 | tf_op jit(solution)/shard_map/psum | solution.py:507
  614.2 152.4 %reduce-scatter.14.cloned.1.call-start = ((), (), s32[]{:S(2)}) async-start(), calls=%async_computation.22 | async-start | bytes 3932160 | tf_op jit(solution)/shard_map/reduce_scatter | solution.py:79
  622.5 6.7 copy-start.14
  (29 other events, 71.4 us)
Sparse Core Ops, SparseCore 0:
  16.7 46.6 all-gather.6
  72.5 19.0 reduce-scatter.7
  145.4 9.9 all-gather.8
  160.0 56.0 reduce-scatter.9
  458.8 42.0 all-gather.14
  506.2 12.0 reduce-scatter.11
  565.0 14.6 all-gather.16
Sparse Core Ops, SparseCore 1:
  162.2 46.9 all-gather.10
  211.0 38.7 all-gather.12
  601.2 75.7 reduce-scatter.15
  680.1 39.7 all-reduce.4
  723.2 43.3 reduce-scatter.13

commit v2 on v1

--- a/solution.py
+++ b/solution.py
@@ -458,14 +458,7 @@
     grad_pre = gelu_pull(grad_active)[0].astype(jnp.bfloat16)
     grad_first = contract_rows(active, grad_received)
     grad_second = contract_rows(grad_pre, received)
-    stacked = lax.psum_scatter(
-        jnp.concatenate([grad_first, grad_second], axis=1).astype(jnp.bfloat16),
-        ("tp", "dp"),
-        scatter_dimension=0,
-        tiled=True,
-    ).astype(jnp.float32)
-    grad_weight_out = stacked[:, :model_width]
-    grad_weight_in = jnp.transpose(stacked[:, model_width:])
+    stacked_in = jnp.concatenate([grad_first, grad_second], axis=1).astype(jnp.bfloat16)
     grad_sent = contract_cols(grad_pre, full_in[0])
     grad_expert_part = jnp.take(return_tokens(grad_sent.astype(jnp.bfloat16)), position, axis=0)
     grad_router_probs = grad_gate * route_hot
@@ -480,11 +473,15 @@
     grad_attn_cols = gather_group(split_columns(grad_low))
     grad_out_weight = contract_rows(attended_group, grad_attn_cols)
     grad_attended = sum_halves(row_product(grad_attn_cols, out_weight, True), group_span)
+    grad_attended, stacked_in = lax.optimization_barrier(
+        (grad_attended.astype(jnp.bfloat16), stacked_in)
+    )
+    stacked = lax.psum_scatter(stacked_in, ("tp", "dp"), scatter_dimension=0, tiled=True)
     grad_qkv, tile_sums = attention_backward(
         ranges,
         qkv_t,
         qkv,
-        grad_attended.astype(jnp.bfloat16),
+        grad_attended,
         attended_t,
         log_sums,
         sequence,
@@ -493,10 +490,23 @@
         block_rows,
     )
     grad_table_local = table_gradient(tile_sums, block_rows)
+    grad_qkv, stacked = lax.optimization_barrier((grad_qkv, stacked))
+    stacked = stacked.astype(jnp.float32)
+    grad_weight_out = stacked[:, :model_width]
+    grad_weight_in = jnp.transpose(stacked[:, model_width:])
     grad_qkv_group = gather_halves(grad_qkv)
     grad_qkv_weight = contract_rows(group_normed, grad_qkv_group)
     grad_normed = join_rows(sum_blocks(row_product(grad_qkv_group, qkv_weight, True), pair_rows))
-    grad_x_norm, grad_gain_one = norm1_pull(grad_normed)
+    grad_x_norm, _ = norm1_pull(grad_normed)
+    gain_part = jnp.sum(grad_qkv_weight * qkv_weight.astype(jnp.float32), axis=1)
+    grad_gain_one = (
+        lax.dynamic_update_slice(
+            jnp.zeros((model_width,), jnp.float32),
+            gain_part,
+            (lax.axis_index("dp") * gain_part.shape[0],),
+        )
+        / norm1_gain
+    )
     grad_in = grad_hidden + grad_x_norm
     table_full = lax.dynamic_update_slice(
         jnp.zeros(bias_table.shape, jnp.float32),

time: 826 us -> 761 us (0.921)
  waiting for transfers between devices: 381 us -> 326 us
  Pallas kernels: 81.2 us -> 63.6 us
    reduce_scatter x2, waiting for transfers between devices: 90 us -> 47 us  [sum_blocks(): lax.psum_scatter(product(jnp.int32(0), lax.axis_size('tp') * row_count).a...]
    psum x1, waiting for transfers between devices: 38.5 us -> 0.01 us  [shards(): lax.psum(grad_qkv_weight.astype(jnp.bfloat16), 'ep').astype(jnp.float32)]
    all_gather x2, waiting for transfers between devices: 10.1 us -> 36.7 us  [gather_halves(): return lax.all_gather(values, 'dp', axis=0, tiled=True)]
    unnamed x13, waiting for transfers between devices: 29.5 us -> 41.3 us
    reduce_scatter x2, waiting for transfers between devices: 15 us -> 3.19 us  [sum_halves(): lax.psum_scatter(product(jnp.int32(0), row_count * lax.axis_size('dp')),...]
    pallas_call x1, Pallas kernels: 38.9 us -> 29.7 us  [attention_forward(): pl.pallas_call(functools.partial(attention_forward_kernel, heads, rows),...]
    pallas_call x1, Pallas kernels: 42.2 us -> 33.9 us  [attention_backward(): pl.pallas_call(functools.partial(attention_backward_kernel, heads, rows),...]
    unnamed x79 -> x106, local copies, waits for them, and re-layouts: 25.7 us -> 25.1 us
  transfers between devices with their start and end apart: 15 -> 15, of which waited for: 12 -> 10; matrix products, arithmetic and copies ran while one was open for 16% -> 15% of each run, Pallas kernels for 0% -> 4%
where the time goes in v2:
time: 761 us; the launch traced here: 758 us
  waiting for transfers between devices  326 us (43%)
  matrix products  103 us (14%)
  blocking collectives  102 us (13%)
  other arithmetic  67.8 us (9%)
  local copies, waits for them, and re-layouts  64.5 us (8%)
  Pallas kernels  63.6 us (8%)
  between operations  16.8 us (2%)
  starting transfers between devices  13.6 us (2%)
    all_gather x2, waiting for transfers between devices, gather_group(): return lax.all_gather(values, 'tp', axis=0, tiled=True)  88.8 us
    all_to_all x2, waiting for transfers between devices, return_tokens(): return lax.all_to_all(values, 'ep', split_axis=0, concat_axis=0, tiled=True)  72 us
    reduce_scatter x2, waiting for transfers between devices, sum_blocks(): lax.psum_scatter(product(jnp.int32(0), lax.axis_size('tp') * row_count).a...  47 us
    unnamed x13, waiting for transfers between devices  41.3 us
    psum x1, blocking collectives, shards(): lax.psum((grad_gain_one, grad_gain_two, grad_router, table_full), ('ep',...  41.3 us
    all_to_all x1, blocking collectives, send_experts(): return lax.all_to_all(values, 'ep', split_axis=0, concat_axis=0, tiled=True)  39.2 us
    dot_general x5, matrix products, contract_cols(): lax.dot_general(left, right, (((1,), (1,)), ((), ())), preferred_element_...  37.7 us
    all_to_all x1, waiting for transfers between devices, send_experts(): return lax.all_to_all(values, 'ep', split_axis=0, concat_axis=0, tiled=True)  37.3 us
  transfers between devices with their start and end apart: 15, of which 10 were waited for; matrix products, arithmetic and copies ran while one was open for 15% of the time, Pallas kernels for 4%

profile of v2, /device:TPU:0, one launch (start us, length us, event | category | flops | bytes accessed | tf_op | source)
XLA Modules:
  0.0 757.7 jit_solution(11600571486068056339)
XLA Ops:
  16.7 46.8 %all-gather.7.cloned.1.call-done = bf16[4096,384]{1,0:T(8,128)(2,1)} async-done(((bf16[1024,384]{1,0:T(8,128)(2,1)}), bf16[4096,384]{1,0:T(8,128)(2,1)}) %all-gather.7.cloned.1.call-update) | async-done | bytes 3145744 | tf_op jit(solution)/shard_map/all_gather | solution.py:62
  63.5 9.1 %fusion.96 = f32[4096,576]{1,0:T(8,128)} fusion(bf16[4096,384]{1,0:T(8,128)(2,1)} %all-gather.7.cloned.1.call-done, bf16[384,576]{0,1:T(8,128)(2,1)S(1)} %copy-done.33), kind=kOutput, calls=%fused_computation.280 | convolution fusion | flops 1811939328 | bytes 13025280 | tf_op jit(solution)/shard_map/dot_general | solution.py:52
  104.4 29.7 %attention_forward.1 = (bf16[2048,192]{1,0:T(8,128)(2,1)S(1)}, f32[192,2048]{1,0:T(8,128)S(1)}, f32[3,1,2048]{2,1,0:T(1,128)S(1)}) custom-call(s32[2,8]{1,0:T(2,128)S(1)} %copy-done.8, bf16[576,2048]{1,0:T(8,128)(2,1)S(1)} %copy.90.qkv_t, bf16[2048,576]{1,0:T(8,128)(2,1)} %multiply_convert_fusion.1.qkv, s32[2048,1]{1,0:T(8,128)S(1)} %copy.91.seq_col, ...), custom_call_target="tpu_custom_call" | custom-call | flops 3221225472 | bytes 12582912 | tf_op jit(solution)/shard_map/attention_forward/pallas_call | solution.py:326
  137.0 24.7 %all-gather.9.cloned.1.call-done = bf16[4096,192]{1,0:T(8,128)(2,1)} async-done(((bf16[2048,192]{1,0:T(8,128)(2,1)}), bf16[4096,192]{1,0:T(8,128)(2,1)}) %all-gather.9.cloned.1.call-update) | async-done | bytes 1572880 | tf_op jit(solution)/shard_map/all_gather | solution.py:75
  175.4 47.0 %reduce-scatter.10.cloned.1.call-done = bf16[1024,384]{1,0:T(8,128)(2,1)} async-done(((bf16[4096,384]{1,0:T(8,128)(2,1)}), bf16[1024,384]{1,0:T(8,128)(2,1)}) %reduce-scatter.10.cloned.1.call-update) | async-done | bytes 786448 | tf_op jit(solution)/shard_map/reduce_scatter | solution.py:79
  241.0 37.3 %all-to-all-done.2 = bf16[4,256,768]{2,1,0:T(8,128)(2,1)S(1)} async-done(((bf16[4,256,768]{2,1,0:T(8,128)(2,1)}), bf16[4,256,768]{2,1,0:T(8,128)(2,1)S(1)}, u32[]{:S(2)}, u32[]{:S(2)}) %all-to-all-start.2) | async-done | bytes 1572896 | tf_op jit(solution)/shard_map/all_to_all | solution.py:94
  278.3 10.8 %fusion.12 = f32[1024,3072]{1,0:T(8,128)} fusion(bf16[1024,768]{1,0:T(8,128)(2,1)S(1)} %bitcast.167, bf16[1,768,3072]{2,1,0:T(8,128)(2,1)} %all-gather.11.cloned.1.call-done), kind=kOutput, calls=%fused_computation.31 | convolution fusion | flops 4831838208 | bytes 18874368 | tf_op jit(solution)/shard_map/dot_general | solution.py:448
  289.0 12.5 %fusion.19 = bf16[1024,768]{1,0:T(8,128)(2,1)} fusion(bf16[1,3072,768]{2,1,0:T(8,128)(2,1)} %all-gather.13.cloned.1.call-done, f32[1024,3072]{1,0:T(8,128)} %fusion.12), kind=kOutput, calls=%fused_computation.72 | convolution fusion | flops 4860936192 | bytes 18874368 | tf_op jit(solution)/shard_map/dot_general | solution.py:451
  306.1 36.1 %all-to-all-done.3 = bf16[4,256,768]{2,1,0:T(8,128)(2,1)S(1)} async-done(((bf16[4,256,768]{2,1,0:T(8,128)(2,1)}), bf16[4,256,768]{2,1,0:T(8,128)(2,1)S(1)}, u32[]{:S(2)}, u32[]{:S(2)}) %all-to-all-start.3) | async-done | bytes 1572896 | tf_op jit(solution)/shard_map/all_to_all | solution.py:98
  350.9 39.2 %all_to_all.114 = bf16[4,256,768]{2,1,0:T(8,128)(2,1)S(1)} all-to-all(bf16[4,256,768]{2,1,0:T(8,128)(2,1)S(1)} %bitcast.157), channel_id=1, replica_groups=mesh['ep'=4,'tp'=4,'dp'=2] {'ep'}, dimensions={0} | all-to-all | bytes 3145728 | tf_op jit(solution)/shard_map/all_to_all | solution.py:94
  390.2 16.9 %fusion.3 = bf16[1024,3072]{1,0:T(8,128)(2,1)S(1)} fusion(f32[1024,3072]{1,0:T(8,128)} %fusion.12, bf16[1024,768]{1,0:T(8,128)(2,1)S(1)} %bitcast.169, bf16[1,3072,768]{2,1,0:T(8,128)(2,1)} %all-gather.13.cloned.1.call-done), kind=kOutput, calls=%fused_computation.15 | convolution fusion | flops 4907335680 | bytes 25165824 | tf_op jit(solution)/shard_map/dot_general | solution.py:42
  407.1 6.2 fusion.16
  417.0 35.9 %all-to-all-done.5 = bf16[4,256,768]{2,1,0:T(8,128)(2,1)S(1)} async-done(((bf16[4,256,768]{2,1,0:T(8,128)(2,1)}), bf16[4,256,768]{2,1,0:T(8,128)(2,1)S(1)}, u32[]{:S(2)}, u32[]{:S(2)}) %all-to-all-start.5) | async-done | bytes 1572896 | tf_op jit(solution)/shard_map/all_to_all | solution.py:98
  465.6 42.0 %all-gather.15.cloned.1.call-done = bf16[4096,384]{1,0:T(8,128)(2,1)} async-done(((bf16[1024,384]{1,0:T(8,128)(2,1)}), bf16[4096,384]{1,0:T(8,128)(2,1)}) %all-gather.15.cloned.1.call-update) | async-done | bytes 3145744 | tf_op jit(solution)/shard_map/all_gather | solution.py:62
  514.2 8.2 %convolution_convert_fusion.2 = bf16[3072,768]{0,1:T(8,128)(2,1)S(1)} fusion(bf16[1024,3072]{1,0:T(8,128)(2,1)} %copy-done.49, bf16[1024,768]{1,0:T(8,128)(2,1)S(1)} %bitcast.168), kind=kOutput, calls=%fused_computation.23 | convolution fusion | flops 4834197504 | bytes 12582912 | tf_op jit(solution)/shard_map/dot_general | solution.py:36
  522.4 9.1 %convolution_convert_fusion.3 = bf16[3072,768]{0,1:T(8,128)(2,1)S(1)} fusion(bf16[1024,768]{1,0:T(8,128)(2,1)S(1)} %bitcast.170, f32[1024,3072]{1,0:T(8,128)} %fusion.12), kind=kOutput, calls=%fused_computation.24 | convolution fusion | flops 4862509056 | bytes 18874368 | tf_op jit(solution)/shard_map/dot_general | solution.py:36
  537.6 12.7 %copy.134 = bf16[3072,1536]{1,0:T(8,128)(2,1)} copy(bf16[3072,1536]{0,1:T(8,128)(2,1)} %pad_maximum_fusion) | data formatting | bytes 18874368
  552.9 33.9 %attention_backward.1 = (bf16[2048,576]{1,0:T(8,128)(2,1)}, f32[3,5,256,256]{3,2,1,0:T(8,128)}) custom-call(s32[2,8]{1,0:T(2,128)S(1)} %copy-done.9, bf16[576,2048]{1,0:T(8,128)(2,1)} %copy-done.1, bf16[2048,576]{1,0:T(8,128)(2,1)} %multiply_convert_fusion.1.qkv, bf16[192,2048]{1,0:T(8,128)(2,1)S(1)} %copy.96.grad_t, ...), custom_call_target="tpu_custom_call" | custom-call | flops 8053063680 | bytes 20971520 | tf_op jit(solution)/shard_map/attention_backward/pallas_call | solution.py:350
  586.9 40.3 %reduce-scatter.16.cloned.1.call-done = bf16[384,1536]{1,0:T(8,128)(2,1)} async-done(((bf16[3072,1536]{1,0:T(8,128)(2,1)}), bf16[384,1536]{1,0:T(8,128)(2,1)}) %reduce-scatter.16.cloned.1.call-update) | async-done | bytes 1179664
  632.9 12.0 %all-gather.17.cloned.1.call-done = bf16[4096,576]{1,0:T(8,128)(2,1)} async-done(((bf16[2048,576]{1,0:T(8,128)(2,1)}), bf16[4096,576]{1,0:T(8,128)(2,1)}) %all-gather.17.cloned.1.call-update) | async-done | bytes 4718608 | tf_op jit(solution)/shard_map/all_gather | solution.py:75
  644.9 7.5 fusion.94
  652.7 7.3 convolution_convert_fusion
  660.1 6.5 broadcast_compare_fusion.7
  696.0 41.3 %all-reduce.1 = (f32[768]{0:T(1024)}, f32[32,12]{0,1:T(8,128)}, f32[768]{0:T(1024)}, f32[768,4]{0,1:T(4,128)}) all-reduce(f32[768]{0:T(1024)S(1)} %div.80, f32[32,12]{0,1:T(8,128)S(1)} %dynamic_update_slice.7, f32[768]{0:T(1024)S(1)} %get-tuple-element.105, ...), channel_id=1, replica_groups=mesh['ep'=4,'tp'=4,'dp'=2] {'ep','tp','dp'}, use_global_device_ids=true, to_apply=%region_22.26 | all-reduce | flops 4992 | bytes 39936 | tf_op jit(solution)/shard_map/psum | solution.py:520
  (273 shorter events, 167.9 us)
Async XLA Ops:
  8.0 153.6 %copy-start = (bf16[192,384]{1,0:T(8,128)(2,1)S(1)}, bf16[192,384]{1,0:T(8,128)(2,1)}, u32[]{:S(2)}) copy-start(bf16[192,384]{1,0:T(8,128)(2,1)} %param.22) | copy-start | bytes 442372
  8.0 55.4 %all-gather.7.cloned.1.call-start = ((), (), s32[]{:S(2)}) async-start(), calls=%async_computation.13 | async-start | bytes 3932160 | tf_op jit(solution)/shard_map/all_gather | solution.py:62
  11.3 52.2 %copy-start.33 = (bf16[384,576]{0,1:T(8,128)(2,1)S(1)}, bf16[384,576]{0,1:T(8,128)(2,1)}, u32[]{:S(2)}) copy-start(bf16[384,576]{0,1:T(8,128)(2,1)} %param.21) | copy-start | bytes 1327108
  16.7 75.1 %reduce-scatter.8.cloned.1.call-start = ((), (), s32[]{:S(2)}) async-start(), calls=%async_computation.14 | async-start | bytes 15728640 | tf_op jit(solution)/shard_map/reduce_scatter | solution.py:66
  72.6 89.1 %all-gather.9.cloned.1.call-start = ((), (), s32[]{:S(2)}) async-start(), calls=%async_computation.15 | async-start | bytes 3145728 | tf_op jit(solution)/shard_map/all_gather | solution.py:75
  74.1 30.3 %copy-start.2 = (s32[2048,1]{1,0:T(8,128)}, s32[2048,1]{1,0:T(8,128)S(1)}, u32[]{:S(2)}) copy-start(s32[2048,1]{1,0:T(8,128)S(1)} %copy.91.seq_col) | copy-start | bytes 24580
  136.9 85.5 %reduce-scatter.10.cloned.1.call-start = ((), (), s32[]{:S(2)}) async-start(), calls=%async_computation.16 | async-start | bytes 3932160 | tf_op jit(solution)/shard_map/reduce_scatter | solution.py:79
  166.2 74.8 %all-gather.11.cloned.1.call-start = ((), (), s32[]{:S(2)}) async-start(), calls=%async_computation.17 | async-start | bytes 5308416 | tf_op jit(solution)/shard_map/all_gather | solution.py:445
  166.8 122.3 %all-gather.13.cloned.1.call-start = ((), (), s32[]{:S(2)}) async-start(), calls=%async_computation.18 | async-start | bytes 5308416 | tf_op jit(solution)/shard_map/all_gather | solution.py:446
  230.9 74.9 %copy-start.14 = (bf16[512,768]{1,0:T(8,128)(2,1)}, bf16[512,768]{1,0:T(8,128)(2,1)S(1)}, u32[]{:S(2)}) copy-start(bf16[512,768]{1,0:T(8,128)(2,1)S(1)} %multiply_convert_fusion.3) | copy-start | bytes 2359300
  236.4 41.9 %all-to-all-start.2 = ((bf16[4,256,768]{2,1,0:T(8,128)(2,1)}), bf16[4,256,768]{2,1,0:T(8,128)(2,1)S(1)}, u32[]{:S(2)}, u32[]{:S(2)}) async-start(bf16[4,256,768]{2,1,0:T(8,128)(2,1)} %bitcast.20), calls=%async_computation.4 | async-start | bytes 3145728 | tf_op jit(solution)/shard_map/all_to_all | solution.py:94
  301.6 40.6 %all-to-all-start.3 = ((bf16[4,256,768]{2,1,0:T(8,128)(2,1)}), bf16[4,256,768]{2,1,0:T(8,128)(2,1)S(1)}, u32[]{:S(2)}, u32[]{:S(2)}) async-start(bf16[4,256,768]{2,1,0:T(8,128)(2,1)} %bitcast.171), calls=%async_computation.5 | async-start | bytes 3145728 | tf_op jit(solution)/shard_map/all_to_all | solution.py:98
  350.9 56.1 %slice-start = ((s8[4718592]{0:T(1024)(128)(4,1)}), s8[4194304]{0:T(1024)(128)(4,1)S(1)}, s32[]{:S(2)}) async-start(s8[4718592]{0:T(1024)(128)(4,1)} %bitcast.214), calls=%async_computation.25 | async-start | bytes 8388608
  390.1 16.9 %copy-start.31 = (bf16[4,256,768]{2,1,0:T(8,128)(2,1)}, bf16[4,256,768]{2,1,0:T(8,128)(2,1)S(1)}, u32[]{:S(2)}) copy-start(bf16[4,256,768]{2,1,0:T(8,128)(2,1)S(1)} %all_to_all.114) | copy-start | bytes 4718596
  390.1 16.9 %slice-start.1 = ((s8[4718592]{0:T(1024)(128)(4,1)}), s8[524288]{0:T(1024)(128)(4,1)S(1)}, s32[]{:S(2)}) async-start(s8[4718592]{0:T(1024)(128)(4,1)} %bitcast.214), calls=%async_computation.26 | async-start | bytes 1048576
  413.3 39.6 %all-to-all-start.5 = ((bf16[4,256,768]{2,1,0:T(8,128)(2,1)}), bf16[4,256,768]{2,1,0:T(8,128)(2,1)S(1)}, u32[]{:S(2)}, u32[]{:S(2)}) async-start(bf16[4,256,768]{2,1,0:T(8,128)(2,1)} %bitcast.28), calls=%async_computation.7 | async-start | bytes 3145728 | tf_op jit(solution)/shard_map/all_to_all | solution.py:98
  416.9 90.7 %all-gather.15.cloned.1.call-start = ((), (), s32[]{:S(2)}) async-start(), calls=%async_computation.19 | async-start | bytes 3932160 | tf_op jit(solution)/shard_map/all_gather | solution.py:62
  465.3 70.6 %reduce-scatter.12.cloned.1.call-start = ((), (), s32[]{:S(2)}) async-start(), calls=%async_computation.20 | async-start | bytes 6291456 | tf_op jit(solution)/shard_map/reduce_scatter | solution.py:66
  512.8 114.4 %reduce-scatter.16.cloned.1.call-start = ((), (), s32[]{:S(2)}) async-start(), calls=%async_computation.23 | async-start | bytes 10616832
  550.3 94.6 %all-gather.17.cloned.1.call-start = ((), (), s32[]{:S(2)}) async-start(), calls=%async_computation.21 | async-start | bytes 7864320 | tf_op jit(solution)/shard_map/all_gather | solution.py:75
  586.8 42.8 %copy-start.27 = (bf16[4096,384]{1,0:T(8,128)(2,1)S(1)}, bf16[4096,384]{1,0:T(8,128)(2,1)}, u32[]{:S(2)}) copy-start(bf16[4096,384]{1,0:T(8,128)(2,1)} %all-gather.15.cloned.1.call-done) | copy-start | bytes 9437188
  629.6 107.7 %all-reduce.5.cloned.1.call-start = ((), (), s32[]{:S(2)}) async-start(), calls=%async_computation.24 | async-start | bytes 1179648 | tf_op jit(solution)/shard_map/psum | solution.py:517
  632.9 19.8 %copy-start.34 = (bf16[384,576]{0,1:T(8,128)(2,1)S(1)}, bf16[384,576]{0,1:T(8,128)(2,1)}, u32[]{:S(2)}) copy-start(bf16[384,576]{0,1:T(8,128)(2,1)} %param.21) | copy-start | bytes 1327108
  652.4 88.5 %reduce-scatter.14.cloned.1.call-start = ((), (), s32[]{:S(2)}) async-start(), calls=%async_computation.22 | async-start | bytes 3932160 | tf_op jit(solution)/shard_map/reduce_scatter | solution.py:79
  (43 other events, 158.5 us)
Sparse Core Ops, SparseCore 0:
  16.8 46.6 all-gather.6
  72.7 19.0 reduce-scatter.7
  137.0 24.5 all-gather.8
  166.3 56.0 reduce-scatter.9
  465.4 42.0 all-gather.14
  512.9 12.0 reduce-scatter.11
  629.7 15.1 all-gather.16
  660.2 45.4 reduce-scatter.13
Sparse Core Ops, SparseCore 1:
  168.5 46.9 all-gather.10
  217.3 38.7 all-gather.12
  550.4 76.7 reduce-scatter.15
  652.5 41.0 all-reduce.4

commit v3 on v2

--- a/solution.py
+++ b/solution.py
@@ -471,6 +471,7 @@
     grad_hidden = grad_out + grad_hidden_norm
     grad_low = grad_hidden.astype(jnp.bfloat16)
     grad_attn_cols = gather_group(split_columns(grad_low))
+    grad_attn_cols, stacked_in = lax.optimization_barrier((grad_attn_cols, stacked_in))
     grad_out_weight = contract_rows(attended_group, grad_attn_cols)
     grad_attended = sum_halves(row_product(grad_attn_cols, out_weight, True), group_span)
     grad_attended, stacked_in = lax.optimization_barrier(

time: 761 us -> 752 us (0.988)
  waiting for transfers between devices: 326 us -> 300 us
  Pallas kernels: 63.6 us -> 81.1 us
    all_gather x2, waiting for transfers between devices: 88.8 us -> 67.3 us  [gather_group(): return lax.all_gather(values, 'tp', axis=0, tiled=True)]
    reduce_scatter x2, waiting for transfers between devices: 3.19 us -> 15.3 us  [sum_halves(): lax.psum_scatter(product(jnp.int32(0), row_count * lax.axis_size('dp')),...]
    all_gather x2, waiting for transfers between devices: 36.7 us -> 27.5 us  [gather_halves(): return lax.all_gather(values, 'dp', axis=0, tiled=True)]
    pallas_call x1, Pallas kernels: 29.7 us -> 38.9 us  [attention_forward(): pl.pallas_call(functools.partial(attention_forward_kernel, heads, rows),...]
    pallas_call x1, Pallas kernels: 33.9 us -> 42.1 us  [attention_backward(): pl.pallas_call(functools.partial(attention_backward_kernel, heads, rows),...]
  transfers between devices with their start and end apart: 15 -> 15, of which waited for: 10 -> 11; matrix products, arithmetic and copies ran while one was open for 15% -> 15% of each run, Pallas kernels for 4% -> 6%
where the time goes in v3:
time: 752 us; the launch traced here: 748 us
  waiting for transfers between devices  300 us (40%)
  matrix products  103 us (14%)
  blocking collectives  102 us (14%)
  Pallas kernels  81.1 us (11%)
  other arithmetic  67.9 us (9%)
  local copies, waits for them, and re-layouts  63.2 us (8%)
  between operations  16.8 us (2%)
  starting transfers between devices  13.6 us (2%)
    all_to_all x2, waiting for transfers between devices, return_tokens(): return lax.all_to_all(values, 'ep', split_axis=0, concat_axis=0, tiled=True)  72 us
    all_gather x2, waiting for transfers between devices, gather_group(): return lax.all_gather(values, 'tp', axis=0, tiled=True)  67.3 us
    reduce_scatter x2, waiting for transfers between devices, sum_blocks(): lax.psum_scatter(product(jnp.int32(0), lax.axis_size('tp') * row_count).a...  47 us
    pallas_call x1, Pallas kernels, attention_backward(): pl.pallas_call(functools.partial(attention_backward_kernel, heads, rows),...  42.1 us
    psum x1, blocking collectives, shards(): lax.psum((grad_gain_one, grad_gain_two, grad_router, table_full), ('ep',...  41.4 us
    all_to_all x1, blocking collectives, send_experts(): return lax.all_to_all(values, 'ep', split_axis=0, concat_axis=0, tiled=True)  39.2 us
    pallas_call x1, Pallas kernels, attention_forward(): pl.pallas_call(functools.partial(attention_forward_kernel, heads, rows),...  38.9 us
    dot_general x5, matrix products, contract_cols(): lax.dot_general(left, right, (((1,), (1,)), ((), ())), preferred_element_...  37.6 us
  transfers between devices with their start and end apart: 15, of which 11 were waited for; matrix products, arithmetic and copies ran while one was open for 15% of the time, Pallas kernels for 6%

profile of v3, /device:TPU:0, one launch (start us, length us, event | category | flops | bytes accessed | tf_op | source)
XLA Modules:
  0.0 747.7 jit_solution(8561216473976695826)
XLA Ops:
  16.7 46.8 %all-gather.7.cloned.1.call-done = bf16[4096,384]{1,0:T(8,128)(2,1)} async-done(((bf16[1024,384]{1,0:T(8,128)(2,1)}), bf16[4096,384]{1,0:T(8,128)(2,1)}) %all-gather.7.cloned.1.call-update) | async-done | bytes 3145744 | tf_op jit(solution)/shard_map/all_gather | solution.py:62
  63.5 9.1 %fusion.96 = f32[4096,576]{1,0:T(8,128)} fusion(bf16[4096,384]{1,0:T(8,128)(2,1)} %all-gather.7.cloned.1.call-done, bf16[384,576]{0,1:T(8,128)(2,1)S(1)} %copy-done.33), kind=kOutput, calls=%fused_computation.280 | convolution fusion | flops 1811939328 | bytes 13025280 | tf_op jit(solution)/shard_map/dot_general | solution.py:52
  104.4 38.9 %attention_forward.1 = (bf16[2048,192]{1,0:T(8,128)(2,1)S(1)}, f32[192,2048]{1,0:T(8,128)S(1)}, f32[3,1,2048]{2,1,0:T(1,128)S(1)}) custom-call(s32[2,8]{1,0:T(2,128)S(1)} %copy-done.8, bf16[576,2048]{1,0:T(8,128)(2,1)S(1)} %copy.90.qkv_t, bf16[2048,576]{1,0:T(8,128)(2,1)} %multiply_convert_fusion.1.qkv, s32[2048,1]{1,0:T(8,128)S(1)} %copy.91.seq_col, ...), custom_call_target="tpu_custom_call" | custom-call | flops 3221225472 | bytes 12582912 | tf_op jit(solution)/shard_map/attention_forward/pallas_call | solution.py:326
  146.2 15.5 %all-gather.9.cloned.1.call-done = bf16[4096,192]{1,0:T(8,128)(2,1)} async-done(((bf16[2048,192]{1,0:T(8,128)(2,1)}), bf16[4096,192]{1,0:T(8,128)(2,1)}) %all-gather.9.cloned.1.call-update) | async-done | bytes 1572880 | tf_op jit(solution)/shard_map/all_gather | solution.py:75
  175.4 47.0 %reduce-scatter.10.cloned.1.call-done = bf16[1024,384]{1,0:T(8,128)(2,1)} async-done(((bf16[4096,384]{1,0:T(8,128)(2,1)}), bf16[1024,384]{1,0:T(8,128)(2,1)}) %reduce-scatter.10.cloned.1.call-update) | async-done | bytes 786448 | tf_op jit(solution)/shard_map/reduce_scatter | solution.py:79
  241.0 37.3 %all-to-all-done.2 = bf16[4,256,768]{2,1,0:T(8,128)(2,1)S(1)} async-done(((bf16[4,256,768]{2,1,0:T(8,128)(2,1)}), bf16[4,256,768]{2,1,0:T(8,128)(2,1)S(1)}, u32[]{:S(2)}, u32[]{:S(2)}) %all-to-all-start.2) | async-done | bytes 1572896 | tf_op jit(solution)/shard_map/all_to_all | solution.py:94
  278.3 10.8 %fusion.12 = f32[1024,3072]{1,0:T(8,128)} fusion(bf16[1024,768]{1,0:T(8,128)(2,1)S(1)} %bitcast.167, bf16[1,768,3072]{2,1,0:T(8,128)(2,1)} %all-gather.11.cloned.1.call-done), kind=kOutput, calls=%fused_computation.31 | convolution fusion | flops 4831838208 | bytes 18874368 | tf_op jit(solution)/shard_map/dot_general | solution.py:448
  289.1 12.5 %fusion.19 = bf16[1024,768]{1,0:T(8,128)(2,1)} fusion(bf16[1,3072,768]{2,1,0:T(8,128)(2,1)} %all-gather.13.cloned.1.call-done, f32[1024,3072]{1,0:T(8,128)} %fusion.12), kind=kOutput, calls=%fused_computation.72 | convolution fusion | flops 4860936192 | bytes 18874368 | tf_op jit(solution)/shard_map/dot_general | solution.py:451
  306.2 36.1 %all-to-all-done.3 = bf16[4,256,768]{2,1,0:T(8,128)(2,1)S(1)} async-done(((bf16[4,256,768]{2,1,0:T(8,128)(2,1)}), bf16[4,256,768]{2,1,0:T(8,128)(2,1)S(1)}, u32[]{:S(2)}, u32[]{:S(2)}) %all-to-all-start.3) | async-done | bytes 1572896 | tf_op jit(solution)/shard_map/all_to_all | solution.py:98
  350.9 39.2 %all_to_all.114 = bf16[4,256,768]{2,1,0:T(8,128)(2,1)S(1)} all-to-all(bf16[4,256,768]{2,1,0:T(8,128)(2,1)S(1)} %bitcast.157), channel_id=1, replica_groups=mesh['ep'=4,'tp'=4,'dp'=2] {'ep'}, dimensions={0} | all-to-all | bytes 3145728 | tf_op jit(solution)/shard_map/all_to_all | solution.py:94
  390.2 16.9 %fusion.3 = bf16[1024,3072]{1,0:T(8,128)(2,1)S(1)} fusion(f32[1024,3072]{1,0:T(8,128)} %fusion.12, bf16[1024,768]{1,0:T(8,128)(2,1)S(1)} %bitcast.169, bf16[1,3072,768]{2,1,0:T(8,128)(2,1)} %all-gather.13.cloned.1.call-done), kind=kOutput, calls=%fused_computation.15 | convolution fusion | flops 4907335680 | bytes 25165824 | tf_op jit(solution)/shard_map/dot_general | solution.py:42
  417.0 35.9 %all-to-all-done.5 = bf16[4,256,768]{2,1,0:T(8,128)(2,1)S(1)} async-done(((bf16[4,256,768]{2,1,0:T(8,128)(2,1)}), bf16[4,256,768]{2,1,0:T(8,128)(2,1)S(1)}, u32[]{:S(2)}, u32[]{:S(2)}) %all-to-all-start.5) | async-done | bytes 1572896 | tf_op jit(solution)/shard_map/all_to_all | solution.py:98
  465.7 8.3 %convolution_convert_fusion.2 = bf16[3072,768]{0,1:T(8,128)(2,1)S(1)} fusion(bf16[1024,3072]{1,0:T(8,128)(2,1)} %copy-done.49, bf16[1024,768]{1,0:T(8,128)(2,1)S(1)} %bitcast.168), kind=kOutput, calls=%fused_computation.23 | convolution fusion | flops 4834197504 | bytes 12582912 | tf_op jit(solution)/shard_map/dot_general | solution.py:36
  474.1 8.7 %convolution_convert_fusion.3 = bf16[3072,768]{0,1:T(8,128)(2,1)S(1)} fusion(bf16[1024,768]{1,0:T(8,128)(2,1)S(1)} %bitcast.170, f32[1024,3072]{1,0:T(8,128)} %fusion.12), kind=kOutput, calls=%fused_computation.24 | convolution fusion | flops 4862509056 | bytes 18874368 | tf_op jit(solution)/shard_map/dot_general | solution.py:36
  487.2 20.6 %all-gather.15.cloned.1.call-done = bf16[4096,384]{1,0:T(8,128)(2,1)} async-done(((bf16[1024,384]{1,0:T(8,128)(2,1)}), bf16[4096,384]{1,0:T(8,128)(2,1)}) %all-gather.15.cloned.1.call-update) | async-done | bytes 3145744 | tf_op jit(solution)/shard_map/all_gather | solution.py:62
  512.9 12.1 %reduce-scatter.12.cloned.1.call-done = f32[2048,192]{1,0:T(8,128)} async-done(((f32[4096,192]{1,0:T(8,128)}), f32[2048,192]{1,0:T(8,128)}) %reduce-scatter.12.cloned.1.call-update) | async-done | bytes 1572880 | tf_op jit(solution)/shard_map/reduce_scatter | solution.py:66
  526.7 12.7 %copy.134 = bf16[3072,1536]{1,0:T(8,128)(2,1)} copy(bf16[3072,1536]{0,1:T(8,128)(2,1)} %pad_maximum_fusion) | data formatting | bytes 18874368
  542.1 42.1 %attention_backward.1 = (bf16[2048,576]{1,0:T(8,128)(2,1)}, f32[3,5,256,256]{3,2,1,0:T(8,128)}) custom-call(s32[2,8]{1,0:T(2,128)S(1)} %copy-done.9, bf16[576,2048]{1,0:T(8,128)(2,1)} %copy-done.1, bf16[2048,576]{1,0:T(8,128)(2,1)} %multiply_convert_fusion.1.qkv, bf16[192,2048]{1,0:T(8,128)(2,1)S(1)} %copy.96.grad_t, ...), custom_call_target="tpu_custom_call" | custom-call | flops 8053063680 | bytes 20971520 | tf_op jit(solution)/shard_map/attention_backward/pallas_call | solution.py:350
  584.2 33.0 %reduce-scatter.16.cloned.1.call-done = bf16[384,1536]{1,0:T(8,128)(2,1)} async-done(((bf16[3072,1536]{1,0:T(8,128)(2,1)}), bf16[384,1536]{1,0:T(8,128)(2,1)}) %reduce-scatter.16.cloned.1.call-update) | async-done | bytes 1179664
  622.9 12.0 %all-gather.17.cloned.1.call-done = bf16[4096,576]{1,0:T(8,128)(2,1)} async-done(((bf16[2048,576]{1,0:T(8,128)(2,1)}), bf16[4096,576]{1,0:T(8,128)(2,1)}) %all-gather.17.cloned.1.call-update) | async-done | bytes 4718608 | tf_op jit(solution)/shard_map/all_gather | solution.py:75
  634.9 7.5 %fusion.94 = (bf16[384,576]{0,1:T(8,128)(2,1)}, f32[384]{0:T(512)}) fusion(bf16[384,576]{0,1:T(8,128)(2,1)} %param.21, bf16[4096,384]{1,0:T(8,128)(2,1)} %all-gather.7.cloned.1.call-done, bf16[4096,576]{1,0:T(8,128)(2,1)} %all-gather.17.cloned.1.call-done), kind=kOutput, calls=%fused_computation.278 | convolution fusion | flops 1812823680 | bytes 8750592 | tf_op jit(solution)/shard_map/dot_general | solution.py:36
  642.7 7.3 convolution_convert_fusion
  650.1 6.5 broadcast_compare_fusion.7
  686.0 41.4 %all-reduce.1 = (f32[768]{0:T(1024)}, f32[32,12]{0,1:T(8,128)}, f32[768]{0:T(1024)}, f32[768,4]{0,1:T(4,128)}) all-reduce(f32[768]{0:T(1024)S(1)} %div.80, f32[32,12]{0,1:T(8,128)S(1)} %dynamic_update_slice.7, f32[768]{0:T(1024)S(1)} %get-tuple-element.109, ...), channel_id=1, replica_groups=mesh['ep'=4,'tp'=4,'dp'=2] {'ep','tp','dp'}, use_global_device_ids=true, to_apply=%region_22.26 | all-reduce | flops 4992 | bytes 39936 | tf_op jit(solution)/shard_map/psum | solution.py:521
  (273 shorter events, 172.8 us)
Async XLA Ops:
  8.0 153.7 %copy-start = (bf16[192,384]{1,0:T(8,128)(2,1)S(1)}, bf16[192,384]{1,0:T(8,128)(2,1)}, u32[]{:S(2)}) copy-start(bf16[192,384]{1,0:T(8,128)(2,1)} %param.22) | copy-start | bytes 442372
  8.0 55.5 %all-gather.7.cloned.1.call-start = ((), (), s32[]{:S(2)}) async-start(), calls=%async_computation.13 | async-start | bytes 3932160 | tf_op jit(solution)/shard_map/all_gather | solution.py:62
  11.3 52.2 %copy-start.33 = (bf16[384,576]{0,1:T(8,128)(2,1)S(1)}, bf16[384,576]{0,1:T(8,128)(2,1)}, u32[]{:S(2)}) copy-start(bf16[384,576]{0,1:T(8,128)(2,1)} %param.21) | copy-start | bytes 1327108
  16.7 75.1 %reduce-scatter.8.cloned.1.call-start = ((), (), s32[]{:S(2)}) async-start(), calls=%async_computation.14 | async-start | bytes 15728640 | tf_op jit(solution)/shard_map/reduce_scatter | solution.py:66
  72.6 89.1 %all-gather.9.cloned.1.call-start = ((), (), s32[]{:S(2)}) async-start(), calls=%async_computation.15 | async-start | bytes 3145728 | tf_op jit(solution)/shard_map/all_gather | solution.py:75
  74.0 30.4 %copy-start.2 = (s32[2048,1]{1,0:T(8,128)}, s32[2048,1]{1,0:T(8,128)S(1)}, u32[]{:S(2)}) copy-start(s32[2048,1]{1,0:T(8,128)S(1)} %copy.91.seq_col) | copy-start | bytes 24580
  146.2 76.2 %reduce-scatter.10.cloned.1.call-start = ((), (), s32[]{:S(2)}) async-start(), calls=%async_computation.16 | async-start | bytes 3932160 | tf_op jit(solution)/shard_map/reduce_scatter | solution.py:79
  166.2 74.8 %all-gather.11.cloned.1.call-start = ((), (), s32[]{:S(2)}) async-start(), calls=%async_computation.17 | async-start | bytes 5308416 | tf_op jit(solution)/shard_map/all_gather | solution.py:445
  166.8 122.3 %all-gather.13.cloned.1.call-start = ((), (), s32[]{:S(2)}) async-start(), calls=%async_computation.18 | async-start | bytes 5308416 | tf_op jit(solution)/shard_map/all_gather | solution.py:446
  230.9 74.9 %copy-start.14 = (bf16[512,768]{1,0:T(8,128)(2,1)}, bf16[512,768]{1,0:T(8,128)(2,1)S(1)}, u32[]{:S(2)}) copy-start(bf16[512,768]{1,0:T(8,128)(2,1)S(1)} %multiply_convert_fusion.3) | copy-start | bytes 2359300
  236.4 41.9 %all-to-all-start.2 = ((bf16[4,256,768]{2,1,0:T(8,128)(2,1)}), bf16[4,256,768]{2,1,0:T(8,128)(2,1)S(1)}, u32[]{:S(2)}, u32[]{:S(2)}) async-start(bf16[4,256,768]{2,1,0:T(8,128)(2,1)} %bitcast.20), calls=%async_computation.4 | async-start | bytes 3145728 | tf_op jit(solution)/shard_map/all_to_all | solution.py:94
  301.6 40.6 %all-to-all-start.3 = ((bf16[4,256,768]{2,1,0:T(8,128)(2,1)}), bf16[4,256,768]{2,1,0:T(8,128)(2,1)S(1)}, u32[]{:S(2)}, u32[]{:S(2)}) async-start(bf16[4,256,768]{2,1,0:T(8,128)(2,1)} %bitcast.171), calls=%async_computation.5 | async-start | bytes 3145728 | tf_op jit(solution)/shard_map/all_to_all | solution.py:98
  350.9 56.1 %slice-start = ((s8[4718592]{0:T(1024)(128)(4,1)}), s8[4194304]{0:T(1024)(128)(4,1)S(1)}, s32[]{:S(2)}) async-start(s8[4718592]{0:T(1024)(128)(4,1)} %bitcast.214), calls=%async_computation.25 | async-start | bytes 8388608
  390.2 16.9 %copy-start.31 = (bf16[4,256,768]{2,1,0:T(8,128)(2,1)}, bf16[4,256,768]{2,1,0:T(8,128)(2,1)S(1)}, u32[]{:S(2)}) copy-start(bf16[4,256,768]{2,1,0:T(8,128)(2,1)S(1)} %all_to_all.114) | copy-start | bytes 4718596
  390.2 16.9 %slice-start.1 = ((s8[4718592]{0:T(1024)(128)(4,1)}), s8[524288]{0:T(1024)(128)(4,1)S(1)}, s32[]{:S(2)}) async-start(s8[4718592]{0:T(1024)(128)(4,1)} %bitcast.214), calls=%async_computation.26 | async-start | bytes 1048576
  413.4 39.6 %all-to-all-start.5 = ((bf16[4,256,768]{2,1,0:T(8,128)(2,1)}), bf16[4,256,768]{2,1,0:T(8,128)(2,1)S(1)}, u32[]{:S(2)}, u32[]{:S(2)}) async-start(bf16[4,256,768]{2,1,0:T(8,128)(2,1)} %bitcast.28), calls=%async_computation.7 | async-start | bytes 3145728 | tf_op jit(solution)/shard_map/all_to_all | solution.py:98
  416.9 90.8 %all-gather.15.cloned.1.call-start = ((), (), s32[]{:S(2)}) async-start(), calls=%async_computation.19 | async-start | bytes 3932160 | tf_op jit(solution)/shard_map/all_gather | solution.py:62
  465.5 59.5 %reduce-scatter.12.cloned.1.call-start = ((), (), s32[]{:S(2)}) async-start(), calls=%async_computation.20 | async-start | bytes 6291456 | tf_op jit(solution)/shard_map/reduce_scatter | solution.py:66
  512.8 104.4 %reduce-scatter.16.cloned.1.call-start = ((), (), s32[]{:S(2)}) async-start(), calls=%async_computation.23 | async-start | bytes 10616832
  539.5 95.5 %all-gather.17.cloned.1.call-start = ((), (), s32[]{:S(2)}) async-start(), calls=%async_computation.21 | async-start | bytes 7864320 | tf_op jit(solution)/shard_map/all_gather | solution.py:75
  584.2 35.4 %copy-start.27 = (bf16[4096,384]{1,0:T(8,128)(2,1)S(1)}, bf16[4096,384]{1,0:T(8,128)(2,1)}, u32[]{:S(2)}) copy-start(bf16[4096,384]{1,0:T(8,128)(2,1)} %all-gather.15.cloned.1.call-done) | copy-start | bytes 9437188
  619.6 107.7 %all-reduce.5.cloned.1.call-start = ((), (), s32[]{:S(2)}) async-start(), calls=%async_computation.24 | async-start | bytes 1179648 | tf_op jit(solution)/shard_map/psum | solution.py:518
  622.9 19.8 %copy-start.34 = (bf16[384,576]{0,1:T(8,128)(2,1)S(1)}, bf16[384,576]{0,1:T(8,128)(2,1)}, u32[]{:S(2)}) copy-start(bf16[384,576]{0,1:T(8,128)(2,1)} %param.21) | copy-start | bytes 1327108
  642.4 88.5 %reduce-scatter.14.cloned.1.call-start = ((), (), s32[]{:S(2)}) async-start(), calls=%async_computation.22 | async-start | bytes 3932160 | tf_op jit(solution)/shard_map/reduce_scatter | solution.py:79
  (43 other events, 161.9 us)
Sparse Core Ops, SparseCore 0:
  16.8 46.6 all-gather.6
  72.7 19.0 reduce-scatter.7
  146.3 15.3 all-gather.8
  166.3 56.0 reduce-scatter.9
  465.6 42.0 all-gather.14
  512.9 12.0 reduce-scatter.11
  619.7 15.1 all-gather.16
  650.1 45.4 reduce-scatter.13
Sparse Core Ops, SparseCore 1:
  168.5 46.9 all-gather.10
  217.3 38.7 all-gather.12
  539.5 77.6 reduce-scatter.15
  642.5 41.0 all-reduce.4
